TPU v7x, 128 devices: a whole 4x4x4 slice. The times are simulated.
128 devices in a mesh: section: 4 (over z_lo, core), fsdp: 32 (over x, y, z_hi).
Axes of the slice: x: 4, y: 4, z: 4 (z_hi: 2, z_lo: 2; z = z_hi * 2 + z_lo), core: 2. Of those that a mesh axis runs over, the one named last changes fastest.
Arguments:
- fwd_input: bfloat16 [4, 4096, 6144], P('section', 'fsdp'), may hold values from -6 to 6
- fwd_routes: int32 [4, 4096, 2], P('section', 'fsdp'), may hold values from 0 to 7, all different within a row; in each aligned block of 128 rows (0 to 127, 128 to 255, ..., all dimensions but the last counted through in order) at most 40 rows name the same one
- fwd_weights: float32 [4, 4096, 2], P('section', 'fsdp'), may hold values from 0.25 to 1
- bwd_input: bfloat16 [4, 4096, 6144], P('section', 'fsdp'), may hold values from -6 to 6
- bwd_routes: int32 [4, 4096, 2], P('section', 'fsdp'), may hold values from 0 to 7, all different within a row; in each aligned block of 128 rows (0 to 127, 128 to 255, ..., all dimensions but the last counted through in order) at most 40 rows name the same one
- bwd_weights: float32 [4, 4096, 2], P('section', 'fsdp'), may hold values from 0.25 to 1
- out_grad: bfloat16 [4, 4096, 6144], P('section', 'fsdp'), may hold values from -6 to 6
- up_weight: bfloat16 [4, 6144, 8192], P('section', None, 'fsdp'), may hold values from -0.078125 to 0.078125
- down_weight: bfloat16 [4, 8192, 6144], P('section', 'fsdp'), may hold values from -0.0625 to 0.0625
Outputs:
- next_input: bfloat16 [4, 4096, 6144], P('section', 'fsdp')
- input_grad: bfloat16 [4, 4096, 6144], P('section', 'fsdp')
- up_grad: bfloat16 [4, 6144, 8192], P('section', None, 'fsdp')
- down_grad: bfloat16 [4, 8192, 6144], P('section', 'fsdp')
Inputs may be any that keep to these rules, and one draw needn't show every extreme that they name: `fwd_routes`: each row names two different experts. Of the 128 rows of one device and one micro-batch, at most 40 name any one expert; in every draw some device's rows name one expert exactly 40 times. `bwd_routes`: as for fwd_routes.
All inputs are finite; a program needn't handle non-finite values.
Results may differ from a plain program's by a relative error of at most 0.015.
Values may be sent and summed in bfloat16 or wider, within the bound.
A program may use at most 192 MiB of HBM per device.

v0:
```python
import jax
import jax.numpy as jnp
from jax import lax
from jax.sharding import PartitionSpec as P

CAP = 40


def from_behind(value, axis, steps):
    count = lax.axis_size(axis)
    pairs = [(source, (source + steps) % count) for source in range(count)]
    return lax.ppermute(value, axis, pairs)


def routing_plan(route_ids, route_weights, expert):
    matches = route_ids == expert
    active = jnp.any(matches, axis=-1)
    chosen = jnp.sum(jnp.where(matches, route_weights, jnp.float32(0.0)), axis=-1)
    ordinal = jnp.cumsum(active.astype(jnp.int32)) - 1
    places = jnp.arange(CAP, dtype=jnp.int32)
    selector = jnp.where((ordinal[None, :] == places[:, None]) & active[None, :], 1.0, 0.0).astype(
        jnp.float32
    )
    return (selector, chosen)


def pack_rows(selector, source):
    packed = jnp.dot(selector.astype(jnp.bfloat16), source, preferred_element_type=jnp.float32)
    return packed.astype(jnp.bfloat16)


def unpack_rows(selector, packed):
    return jnp.dot(
        selector.T, packed, precision=lax.Precision.HIGHEST, preferred_element_type=jnp.float32
    )


def silu_slope(values):
    sigma = jax.nn.sigmoid(values)
    return sigma * (1.0 + values * (1.0 - sigma))


def body(
    fwd_input,
    fwd_routes,
    fwd_weights,
    bwd_input,
    bwd_routes,
    bwd_weights,
    out_grad,
    up_weight,
    down_weight,
):
    expert = lax.axis_index("section")
    upper = up_weight[0]
    lower = down_weight[0]
    forward_rows = fwd_input[0]
    backward_rows = bwd_input[0]
    incoming = out_grad[0]
    select_f, weight_f = routing_plan(fwd_routes[0], fwd_weights[0], expert)
    packed_f = pack_rows(select_f, forward_rows)
    select_b, weight_b = routing_plan(bwd_routes[0], bwd_weights[0], expert)
    packed_b = pack_rows(select_b, backward_rows)
    scaled_grad = (weight_b[:, None] * incoming.astype(jnp.float32)).astype(jnp.bfloat16)
    packed_g = pack_rows(select_b, scaled_grad)
    hidden_f = jax.nn.silu(
        jnp.dot(
            lax.all_gather(packed_f, "fsdp", axis=0, tiled=True),
            upper,
            preferred_element_type=jnp.float32,
        )
    ).astype(jnp.bfloat16)
    gathered_b, gathered_g = (
        lax.all_gather(packed_b, "fsdp", axis=0, tiled=True),
        lax.all_gather(packed_g, "fsdp", axis=0, tiled=True),
    )
    block = hidden_f
    expert_f = lax.psum_scatter(
        jnp.dot(block, lower, preferred_element_type=jnp.float32).astype(jnp.bfloat16),
        "fsdp",
        scatter_dimension=0,
        tiled=True,
    ).astype(jnp.float32)
    section_out = forward_rows.astype(jnp.float32) + weight_f[:, None] * unpack_rows(
        select_f, expert_f
    )
    section_out = section_out.astype(jnp.bfloat16)
    next_input = from_behind(section_out, "section", 1)
    pre_b = jnp.dot(gathered_b, upper, preferred_element_type=jnp.float32)
    hidden_b = jax.nn.silu(pre_b).astype(jnp.bfloat16)
    down_grad = lax.dot_general(
        hidden_b, gathered_g, (((0,), (0,)), ((), ())), preferred_element_type=jnp.float32
    ).astype(jnp.bfloat16)
    back_hidden = lax.dot_general(
        gathered_g, lower, (((1,), (1,)), ((), ())), preferred_element_type=jnp.float32
    )
    pre_grad = (back_hidden * silu_slope(pre_b)).astype(jnp.bfloat16)
    up_grad = lax.dot_general(
        gathered_b, pre_grad, (((0,), (0,)), ((), ())), preferred_element_type=jnp.float32
    ).astype(jnp.bfloat16)
    block = pre_grad
    rows_grad = lax.psum_scatter(
        lax.dot_general(
            block, upper, (((1,), (1,)), ((), ())), preferred_element_type=jnp.float32
        ).astype(jnp.bfloat16),
        "fsdp",
        scatter_dimension=0,
        tiled=True,
    ).astype(jnp.float32)
    input_grad = (incoming.astype(jnp.float32) + unpack_rows(select_b, rows_grad)).astype(
        jnp.bfloat16
    )
    return (next_input[None], input_grad[None], up_grad[None], down_grad[None])


def solution(mesh):
    in_specs = (
        P("section", "fsdp", None),
        P("section", "fsdp", None),
        P("section", "fsdp", None),
        P("section", "fsdp", None),
        P("section", "fsdp", None),
        P("section", "fsdp", None),
        P("section", "fsdp", None),
        P("section", None, "fsdp"),
        P("section", "fsdp", None),
    )
    out_specs = (
        P("section", "fsdp", None),
        P("section", "fsdp", None),
        P("section", None, "fsdp"),
        P("section", "fsdp", None),
    )
    return jax.shard_map(body, mesh=mesh, in_specs=in_specs, out_specs=out_specs, check_vma=False)
```

profile of v0, /device:TPU:1, one launch (start us, length us, event | category | flops | bytes accessed | tf_op | source)
XLA Modules:
  0.0 1014.7 jit_solution(4190049523393215109)
XLA Ops:
  7.2 0.0 copy-start
  7.2 0.0 copy-start.2
  7.2 0.0 copy-start.4
  7.2 0.0 all-gather.4.cloned.1.call-start
  7.3 0.8 fusion.66
  8.1 0.1 copy.15
  8.2 0.2 reduce-window.16
  8.4 0.1 add_reduce_fusion.1
  8.5 2.5 convolution_convert_fusion.6
  11.0 0.0 all-gather.4.cloned.1.call-update
  11.1 0.0 all-gather.8.cloned.1.call-start
  11.1 0.7 fusion.67
  11.8 0.1 copy.16
  11.9 0.2 reduce-window.17
  12.1 0.1 add_reduce_fusion
  12.2 2.5 convolution_convert_fusion.4
  14.8 0.0 all-gather.8.cloned.1.call-update
  14.8 0.0 all-gather.6.cloned.1.call-start
  14.8 0.0 copy-done.2
  14.8 0.0 copy-done.4
  14.9 2.7 convolution_convert_fusion.5
  17.6 0.0 all-gather.6.cloned.1.call-update
  17.6 0.0 reduce-scatter.3.cloned.1.call-start
  17.6 146.7 %all-gather.4.cloned.1.call-done = bf16[1280,6144]{1,0:T(8,128)(2,1)} async-done(((bf16[40,6144]{1,0:T(8,128)(2,1)}), bf16[1280,6144]{1,0:T(8,128)(2,1)}) %all-gather.4.cloned.1.call-update) | async-done | bytes 15728656 | tf_op jit(solution)/shard_map/all_gather | solution.py:68
  164.3 0.0 copy-done
  164.3 8.0 multiply_convert_fusion.1
  172.3 9.6 convolution_convert_fusion.1
  181.9 0.0 reduce-scatter.3.cloned.1.call-update
  181.9 0.2 reduce-scatter.5.cloned.1.call-start
  182.2 133.2 %all-gather.8.cloned.1.call-done = bf16[1280,6144]{1,0:T(8,128)(2,1)} async-done(((bf16[40,6144]{1,0:T(8,128)(2,1)}), bf16[1280,6144]{1,0:T(8,128)(2,1)}) %all-gather.8.cloned.1.call-update) | async-done | bytes 15728656 | tf_op jit(solution)/shard_map/all_gather | solution.py:74
  315.4 8.7 fusion.11
  324.1 142.4 %all-gather.6.cloned.1.call-done = bf16[1280,6144]{1,0:T(8,128)(2,1)} async-done(((bf16[40,6144]{1,0:T(8,128)(2,1)}), bf16[1280,6144]{1,0:T(8,128)(2,1)}) %all-gather.6.cloned.1.call-update) | async-done | bytes 15728656 | tf_op jit(solution)/shard_map/all_gather | solution.py:75
  466.5 12.1 %fusion.18 = bf16[1280,256]{1,0:T(8,128)(2,1)} fusion(bf16[1280,6144]{1,0:T(8,128)(2,1)} %all-gather.6.cloned.1.call-done, bf16[1,256,6144]{2,1,0:T(8,128)(2,1)} %param.17, f32[1280,256]{1,0:T(8,128)} %fusion.11), kind=kOutput, calls=%fused_computation.26 | convolution fusion | flops 4029480960 | bytes 20840448 | tf_op jit(solution)/shard_map/dot_general | solution.py:94
  478.7 8.9 convolution_convert_fusion
  487.5 0.0 copy-start.3
  487.5 0.0 copy-start.5
  487.5 0.0 reduce-scatter.5.cloned.1.call-update
  487.6 0.7 copy-done.3
  488.2 0.0 copy-done.5
  488.3 245.5 %reduce-scatter.3.cloned.1.call-done = bf16[40,6144]{1,0:T(8,128)(2,1)} async-done(((bf16[1280,6144]{1,0:T(8,128)(2,1)}), bf16[40,6144]{1,0:T(8,128)(2,1)}) %reduce-scatter.3.cloned.1.call-update) | async-done | bytes 491536 | tf_op jit(solution)/shard_map/reduce_scatter | solution.py:78
  733.8 0.0 copy-start.6
  733.8 4.4 fusion.3
  738.1 0.0 copy-start.1
  738.1 2.0 collective-permute-start
  740.2 0.0 copy-done.6
  740.2 11.4 %fusion = bf16[1,256,6144]{2,1,0:T(8,128)(2,1)} fusion(bf16[1280,6144]{1,0:T(8,128)(2,1)} %all-gather.6.cloned.1.call-done, f32[1280,256]{1,0:T(8,128)S(1)} %copy-done.6), kind=kOutput, calls=%fused_computation.4 | convolution fusion | flops 4029743104 | bytes 20185088 | tf_op jit(solution)/shard_map/dot_general | solution.py:91
  751.5 0.0 copy-done.1
  751.6 11.9 %fusion.1 = bf16[1,6144,256]{2,1,0:T(8,128)(2,1)} fusion(bf16[1280,6144]{1,0:T(8,128)(2,1)} %all-gather.8.cloned.1.call-done, bf16[1280,256]{1,0:T(8,128)(2,1)S(1)} %copy-done.1), kind=kOutput, calls=%fused_computation.5 | convolution fusion | flops 4028104704 | bytes 19529728 | tf_op jit(solution)/shard_map/dot_general | solution.py:98
  763.4 237.9 %reduce-scatter.5.cloned.1.call-done = bf16[40,6144]{1,0:T(8,128)(2,1)} async-done(((bf16[1280,6144]{1,0:T(8,128)(2,1)}), bf16[40,6144]{1,0:T(8,128)(2,1)}) %reduce-scatter.5.cloned.1.call-update) | async-done | bytes 491536 | tf_op jit(solution)/shard_map/reduce_scatter | solution.py:102
  1001.3 4.2 fusion.5
  1005.5 0.0 collective-permute-done
  1005.5 2.7 copy.18
  (4 shorter events, 0.1 us)
Async XLA Ops:
  7.2 157.1 %copy-start = (bf16[1,6144,256]{2,1,0:T(8,128)(2,1)S(1)}, bf16[1,6144,256]{2,1,0:T(8,128)(2,1)}, u32[]{:S(2)}) copy-start(bf16[1,6144,256]{2,1,0:T(8,128)(2,1)} %param.16) | copy-start | bytes 9437188
  7.2 7.7 copy-start.2
  7.2 7.7 copy-start.4
  7.2 157.1 %all-gather.4.cloned.1.call-start = ((), (), s32[]{:S(2)}) async-start(), calls=%async_computation.2 | async-start | bytes 16220160 | tf_op jit(solution)/shard_map/all_gather | solution.py:68
  11.1 304.3 %all-gather.8.cloned.1.call-start = ((), (), s32[]{:S(2)}) async-start(), calls=%async_computation.5 | async-start | bytes 16220160 | tf_op jit(solution)/shard_map/all_gather | solution.py:74
  14.8 451.7 %all-gather.6.cloned.1.call-start = ((), (), s32[]{:S(2)}) async-start(), calls=%async_computation.4 | async-start | bytes 16220160 | tf_op jit(solution)/shard_map/all_gather | solution.py:75
  17.6 716.2 %reduce-scatter.3.cloned.1.call-start = ((), (), s32[]{:S(2)}) async-start(), calls=%async_computation.3 | async-start | bytes 16220160 | tf_op jit(solution)/shard_map/reduce_scatter | solution.py:78
  181.9 819.3 %reduce-scatter.5.cloned.1.call-start = ((), (), s32[]{:S(2)}) async-start(), calls=%async_computation.6 | async-start | bytes 16220160 | tf_op jit(solution)/shard_map/reduce_scatter | solution.py:102
  487.5 0.7 copy-start.3
  487.5 0.7 copy-start.5
  733.8 6.4 copy-start.6
  738.1 13.4 %copy-start.1 = (bf16[1280,256]{1,0:T(8,128)(2,1)S(1)}, bf16[1280,256]{1,0:T(8,128)(2,1)}, u32[]{:S(2)}) copy-start(bf16[1280,256]{1,0:T(8,128)(2,1)} %fusion.18) | copy-start | bytes 1966084
  738.1 267.4 %collective-permute-start = (bf16[128,6144]{1,0:T(8,128)(2,1)}, bf16[128,6144]{1,0:T(8,128)(2,1)}, u32[]{:S(2)}, u32[]{:S(2)}) collective-permute-start(bf16[128,6144]{1,0:T(8,128)(2,1)} %fusion.3), channel_id=1, source_target_pairs={{0,32},{32,64},{64,96},{96,0},{1,33},{33,65},{65,97},{97,1},{2,34}... | collective-permute-start | bytes 4718600 | tf_op jit(solution)/shard_map/ppermute | solution.py:12
Sparse Core Ops, SparseCore 0:
  11.6 152.6 all-gather.3
  167.8 147.5 all-gather.7
  318.9 147.5 all-gather.5
  471.8 261.9 reduce-scatter.2
  739.0 262.2 reduce-scatter.4
where the time goes:
time: 1020 us; the launch traced here: 1010 us
  waiting for transfers between devices  906 us (89%)
  matrix products  86.9 us (9%)
  between operations  13.9 us (1%)
    reduce_scatter x1, waiting for transfers between devices, body(): lax.psum_scatter(jnp.dot(block, lower, preferred_element_type=jnp.float32...  246 us
    reduce_scatter x1, waiting for transfers between devices, body(): lax.psum_scatter(lax.dot_general(block, upper, (((1,), (1,)), ((), ())),...  238 us
    all_gather x1, waiting for transfers between devices, body(): lax.all_gather(packed_f, 'fsdp', axis=0, tiled=True)  147 us
    all_gather x1, waiting for transfers between devices, body(): lax.all_gather(packed_g, 'fsdp', axis=0, tiled=True)  142 us
    all_gather x1, waiting for transfers between devices, body(): lax.all_gather(packed_b, 'fsdp', axis=0, tiled=True)  133 us
  transfers between devices with their start and end apart: 6, of which 5 were waited for; matrix products, arithmetic and copies ran while one was open for 8% of the time, Pallas kernels for 0%

commit v1 on v0

v1 whole, which is shorter than its diff:
```python
import functools

import jax
import jax.numpy as jnp
from jax import lax
from jax.experimental import pallas as pl
from jax.experimental.pallas import tpu as pltpu
from jax.sharding import PartitionSpec as P

MESH = pl.DeviceIdType.MESH
F32 = jnp.float32
BF16 = jnp.bfloat16

CAP = 40
SLOTS = 48
D = 6144
HALF = D // 2
UNITS = 256
BLOCK = 2 * CAP
COLS = HALF // 2
QUARTER = COLS // 2
TILE = 768

B, G, F = 0, 1, 2


def kernel(
    pb_ref,
    pg_ref,
    pf_ref,
    up_ref,
    down_ref,
    xf_ref,
    fin_ref,
    fout_ref,
    rout_ref,
    ug_ref,
    dg_ref,
    rows,
    wu,
    wd,
    local,
    remote,
    part,
    peer,
    dgs,
    ugs,
    r1,
    r2,
    r3,
    r4,
    ag_send,
    ag_recv,
    rs_send,
    rs_recv,
    pre_send,
    pre_recv,
    z_send,
    z_recv,
    loc_sem,
):
    sec = lax.axis_index("section")
    me = lax.axis_index("fsdp")
    mx = me // 8
    my = (me // 2) % 4
    zh = me % 2
    mate = me + 1 - 2 * zh
    after = (sec + 1) % 4
    before = (sec + 3) % 4

    def at(x, y):
        return (sec, (((x + 4) % 4) * 4 + (y + 4) % 4) * 2 + zh)

    pair = (sec, mate)

    barrier = pltpu.get_barrier_semaphore()
    near = [
        at(mx + 1, my),
        at(mx - 1, my),
        at(mx, my + 1),
        at(mx, my - 1),
        pair,
        (after, me),
        (after, mate),
        (before, me),
        (before, mate),
    ]
    for device in near:
        pl.semaphore_signal(barrier, inc=1, device_id=device, device_id_type=MESH)
    pl.semaphore_wait(barrier, len(near))

    mine = pl.ds(pl.multiple_of(zh * HALF, HALF), HALF)
    other = pl.ds(pl.multiple_of((1 - zh) * HALF, HALF), HALF)
    started = []

    def send(src, dst, send_sem, recv_sem, device):
        copy = pltpu.make_async_remote_copy(
            src_ref=src,
            dst_ref=dst,
            send_sem=send_sem,
            recv_sem=recv_sem,
            device_id=device,
            device_id_type=MESH,
        )
        copy.start()
        return copy

    def keep(src, dst, index):
        copy = pltpu.make_async_copy(src, dst, loc_sem.at[index])
        copy.start()
        return copy

    def zsend(src, dst, index, device=pair):
        return send(src, dst, z_send.at[index], z_recv.at[index], device)

    packed = (pb_ref, pg_ref, pf_ref)
    token = [zsend(packed[s].at[:, other], remote.at[s], s) for s in (B, G, F)]
    own = [keep(packed[s].at[:, mine], local.at[s], s) for s in (B, G, F)]
    wu_in = zsend(up_ref.at[other], wu.at[1], 3)
    wu_own = keep(up_ref.at[mine], wu.at[0], 3)
    wd_own = keep(down_ref.at[:, mine], wd.at[0], 4)

    slot = lax.broadcasted_iota(jnp.int32, (BLOCK, SLOTS), 1)
    row = lax.broadcasted_iota(jnp.int32, (BLOCK, SLOTS), 0)

    def place(which):
        hit = (row == slot + CAP * which) & (slot < CAP)
        return jnp.where(hit, 1.0, 0.0).astype(BF16)

    place_mine, place_other = place(zh), place(1 - zh)

    def fill(s):
        token[s].wait_recv()
        own[s].wait()
        for c in range(0, HALF, TILE):
            cols = pl.ds(c, TILE)
            total = jnp.dot(place_mine, local[s, :, cols], preferred_element_type=F32)
            total += jnp.dot(place_other, remote[s, :, cols], preferred_element_type=F32)
            rows[s, mx, my, :, cols] = total.astype(BF16)

    def up4(i):
        return (i + 4) % 4

    def one(h, i):
        return (up4(i), my) if h == 0 else (mx, up4(i))

    def g1(s, h, i, start, width):
        x, y = one(h, i)
        return rows.at[s, x, y, :, pl.ds(h * COLS + start, width)]

    def g4(s, h, j, start, width):
        cols = pl.ds(h * COLS + start, width)
        if h == 0:
            return rows.at[s, :, up4(j), :, cols]
        return rows.at[s, up4(j), :, :, cols]

    first, second = (mx, my), (my, mx)

    def dev1(h, step):
        return at(mx + step, my) if h == 0 else at(mx, my + step)

    def dev2(h, step):
        return at(mx, my + step) if h == 0 else at(mx + step, my)

    gathers = {}

    def gsend(s, h, k, ref, device):
        gathers[s, h, k] = send(ref, ref, ag_send.at[s, h, k], ag_recv.at[s, h, k], device)

    def gather1(s):
        for h in (0, 1):
            ref = g1(s, h, first[h], 0, COLS)
            gsend(s, h, 0, ref, dev1(h, 1))
            gsend(s, h, 1, ref, dev1(h, -1))

    def gather2(s):
        for h in (0, 1):
            gathers[s, h, 0].wait_recv()
            gsend(s, h, 2, g1(s, h, first[h] - 1, 0, QUARTER), dev1(h, 1))
            gathers[s, h, 1].wait_recv()
            gsend(s, h, 3, g1(s, h, first[h] + 1, QUARTER, QUARTER), dev1(h, -1))

    def gather3(s):
        for h in (0, 1):
            gathers[s, h, 2].wait_recv()
            gathers[s, h, 3].wait_recv()
            ref = g4(s, h, second[h], 0, COLS)
            gsend(s, h, 4, ref, dev2(h, 1))
            gsend(s, h, 5, ref, dev2(h, -1))

    def gather4(s):
        for h in (0, 1):
            gathers[s, h, 4].wait_recv()
            gsend(s, h, 6, g4(s, h, second[h] - 1, 0, QUARTER), dev2(h, 1))
            gathers[s, h, 5].wait_recv()
            gsend(s, h, 7, g4(s, h, second[h] + 1, QUARTER, QUARTER), dev2(h, -1))

    def gather5(s):
        for h in (0, 1):
            gathers[s, h, 6].wait_recv()
            gathers[s, h, 7].wait_recv()

    def gathered_out(s):
        for h in (0, 1):
            for k in range(8):
                gathers[s, h, k].wait_send()

    def pre_copy(s, i):
        return pltpu.make_async_remote_copy(
            src_ref=part.at[s, i],
            dst_ref=peer.at[s, i],
            send_sem=pre_send.at[s, i],
            recv_sem=pre_recv.at[s, i],
            device_id=pair,
            device_id_type=MESH,
        )

    last = (((1,), (1,)), ((), ()))
    lead = (((0,), (0,)), ((), ()))

    def partial_up(s):
        def step(i, carry):
            block = rows[s, i].reshape(4 * BLOCK, HALF)
            for u in (0, 1):
                value = jnp.dot(block, wu[u], preferred_element_type=F32)
                part[s, i, :, pl.ds(u * UNITS, UNITS)] = value.astype(BF16)
            pre_copy(s, i).start()
            return carry

        lax.fori_loop(0, 4, step, 0)

    def partial_back(s):
        def step(i, carry):
            block = rows[s, i].reshape(4 * BLOCK, HALF)
            for u in (0, 1):
                value = lax.dot_general(block, wd[u], last, preferred_element_type=F32)
                part[s, i, :, pl.ds(u * UNITS, UNITS)] = value.astype(BF16)
            pre_copy(s, i).start()
            return carry

        lax.fori_loop(0, 4, step, 0)

    def whole(s, i, u):
        here = part[s, i, :, pl.ds(u * UNITS, UNITS)].astype(F32)
        return here + peer[s, i, :, pl.ds((1 - u) * UNITS, UNITS)].astype(F32)

    def sigmoid(value):
        return 1.0 / (1.0 + jnp.exp(-value))

    def activate_back():
        def step(i, carry):
            pre_copy(B, i).wait_recv()
            pre_copy(G, i).wait_recv()
            hidden, slope = [], []
            for u in (0, 1):
                pre = whole(B, i, u)
                gate = sigmoid(pre)
                hidden.append((pre * gate).astype(BF16))
                back = whole(G, i, u)
                slope.append((back * (gate * (1.0 + pre * (1.0 - gate)))).astype(BF16))
            for u in (0, 1):
                peer[B, i, :, pl.ds(u * UNITS, UNITS)] = hidden[u]
                peer[G, i, :, pl.ds(u * UNITS, UNITS)] = slope[u]
            return carry

        lax.fori_loop(0, 4, step, 0)

    def activate_fwd():
        def step(i, carry):
            pre_copy(F, i).wait_recv()
            hidden = []
            for u in (0, 1):
                pre = whole(F, i, u)
                hidden.append((pre * sigmoid(pre)).astype(BF16))
            for u in (0, 1):
                peer[F, i, :, pl.ds(u * UNITS, UNITS)] = hidden[u]
            return carry

        lax.fori_loop(0, 4, step, 0)

    def down_grad():
        for u in (1, 0):
            def step(c, carry):
                cols = pl.ds(pl.multiple_of(c * TILE, TILE), TILE)
                left = peer[B, :, :, pl.ds(u * UNITS, UNITS)].reshape(16 * BLOCK, UNITS)
                right = rows[G, :, :, :, cols].reshape(16 * BLOCK, TILE)
                value = lax.dot_general(left, right, lead, preferred_element_type=F32)
                dgs[u, :, cols] = value.astype(BF16)
                return carry

            lax.fori_loop(0, HALF // TILE, step, 0)

    def up_grad():
        def step(c, carry):
            cols = pl.ds(pl.multiple_of(c * TILE, TILE), TILE)
            left = rows[B, :, :, :, cols].reshape(16 * BLOCK, TILE)
            for u in (0, 1):
                right = peer[G, :, :, pl.ds(u * UNITS, UNITS)].reshape(16 * BLOCK, UNITS)
                value = lax.dot_general(left, right, lead, preferred_element_type=F32)
                ugs[u, cols, :] = value.astype(BF16)
            return carry

        lax.fori_loop(0, HALF // TILE, step, 0)

    def rows_out(s, source, weights, dims):
        def step(n, carry):
            i = n // (HALF // TILE)
            c = n % (HALF // TILE)
            cols = pl.ds(pl.multiple_of(c * TILE, TILE), TILE)
            total = None
            for u in (0, 1):
                left = peer[source, i, :, pl.ds(u * UNITS, UNITS)]
                right = weights[u, cols, :] if dims == last else weights[u, :, cols]
                if dims == last:
                    value = lax.dot_general(left, right, last, preferred_element_type=F32)
                else:
                    value = jnp.dot(left, right, preferred_element_type=F32)
                total = value if total is None else total + value
            rows[s, i, :, :, cols] = total.astype(BF16).reshape(4, BLOCK, TILE)
            return carry

        lax.fori_loop(0, 4 * (HALF // TILE), step, 0)

    scatters = {}

    def ssend(s, h, k, src, dst, device):
        scatters[s, h, k] = send(src, dst, rs_send.at[s - 1, h, k], rs_recv.at[s - 1, h, k], device)

    def add4(s, h, j, start, width, sources):
        cols = pl.ds(h * COLS + start, width)

        def step(i, carry):
            x, y = (i, up4(j)) if h == 0 else (up4(j), i)
            total = rows[s, x, y, :, cols].astype(F32)
            for source in sources:
                total += source[i].astype(F32)
            rows[s, x, y, :, cols] = total.astype(BF16)
            return carry

        lax.fori_loop(0, 4, step, 0)

    def sum1(s, h, i, start, width, sources):
        x, y = one(h, i)
        total = rows[s, x, y, :, pl.ds(h * COLS + start, width)].astype(F32)
        for source in sources:
            total += source[...].astype(F32)
        rows[s, x, y, :, pl.ds(h * COLS + start, width)] = total.astype(BF16)

    def scatter1(s):
        for h in (0, 1):
            far = second[h] + 2
            ssend(s, h, 0, g4(s, h, far, 0, QUARTER), r1.at[s - 1, h, 0], dev2(h, 1))
            ssend(s, h, 1, g4(s, h, far, QUARTER, QUARTER), r1.at[s - 1, h, 1], dev2(h, -1))

    def scatter2(s):
        for h in (0, 1):
            scatters[s, h, 0].wait_recv()
            add4(s, h, second[h] + 1, 0, QUARTER, [r1.at[s - 1, h, 0]])
            ssend(s, h, 2, g4(s, h, second[h] + 1, 0, COLS), r2.at[s - 1, h, 0], dev2(h, 1))
            scatters[s, h, 1].wait_recv()
            add4(s, h, second[h] - 1, QUARTER, QUARTER, [r1.at[s - 1, h, 1]])
            ssend(s, h, 3, g4(s, h, second[h] - 1, 0, COLS), r2.at[s - 1, h, 1], dev2(h, -1))

    def scatter3(s):
        for h in (0, 1):
            scatters[s, h, 2].wait_recv()
            scatters[s, h, 3].wait_recv()
            add4(s, h, second[h], 0, COLS, [r2.at[s - 1, h, 0], r2.at[s - 1, h, 1]])
            far = first[h] + 2
            ssend(s, h, 4, g1(s, h, far, 0, QUARTER), r3.at[s - 1, h, 0], dev1(h, 1))
            ssend(s, h, 5, g1(s, h, far, QUARTER, QUARTER), r3.at[s - 1, h, 1], dev1(h, -1))

    def scatter4(s):
        for h in (0, 1):
            scatters[s, h, 4].wait_recv()
            sum1(s, h, first[h] + 1, 0, QUARTER, [r3.at[s - 1, h, 0]])
            ssend(s, h, 6, g1(s, h, first[h] + 1, 0, COLS), r4.at[s - 1, h, 0], dev1(h, 1))
            scatters[s, h, 5].wait_recv()
            sum1(s, h, first[h] - 1, QUARTER, QUARTER, [r3.at[s - 1, h, 1]])
            ssend(s, h, 7, g1(s, h, first[h] - 1, 0, COLS), r4.at[s - 1, h, 1], dev1(h, -1))

    def scatter5(s, mine_ref, other_ref):
        for h in (0, 1):
            scatters[s, h, 6].wait_recv()
            scatters[s, h, 7].wait_recv()
            sum1(s, h, first[h], 0, COLS, [r4.at[s - 1, h, 0], r4.at[s - 1, h, 1]])
        for c in range(0, HALF, TILE):
            cols = pl.ds(c, TILE)
            block = rows[s, mx, my, :, cols]
            mine_ref[:, cols] = lax.dot_general(
                place_mine, block, lead, preferred_element_type=F32
            ).astype(BF16)
            other_ref[:, cols] = lax.dot_general(
                place_other, block, lead, preferred_element_type=F32
            ).astype(BF16)

    fill(B)
    gather1(B)
    gather2(B)
    gather3(B)
    wd_in = zsend(down_ref.at[:, other], wd.at[1], 4)
    fill(G)
    gather1(G)
    gather2(G)
    gather4(B)
    gather3(G)
    fill(F)
    gather1(F)
    gather5(B)
    wu_in.wait_recv()
    wu_own.wait()
    partial_up(B)
    gather4(G)
    gather2(F)
    gather3(F)
    fin = zsend(xf_ref, fin_ref, 10, (after, me))
    gather5(G)
    wd_in.wait_recv()
    wd_own.wait()
    partial_back(G)
    gather4(F)
    gather5(F)
    partial_up(F)
    activate_back()
    down_grad()
    dg_out = zsend(dgs.at[1], dg_ref.at[:, mine], 5)
    dg_own = keep(dgs.at[0], dg_ref.at[:, mine], 5)
    gathered_out(G)
    rows_out(G, G, wu, last)
    scatter1(G)
    up_grad()
    ug_out = zsend(ugs.at[1], ug_ref.at[mine], 6)
    ug_own = keep(ugs.at[0], ug_ref.at[mine], 6)
    scatter2(G)
    activate_fwd()
    gathered_out(F)
    rows_out(F, F, wd, None)
    scatter1(F)
    scatter3(G)
    scatter2(F)
    scatter4(G)
    scatter3(F)
    token[B].wait_send()
    token[G].wait_send()
    token[F].wait_send()
    scatter5(G, local.at[0], local.at[1])
    row_own = keep(local.at[0], rout_ref.at[zh], 7)
    row_out = zsend(local.at[1], rout_ref.at[zh], 7)
    scatter4(F)
    scatter5(F, local.at[2], remote.at[0])
    near_out = zsend(local.at[2], fout_ref.at[zh], 8, (after, me))
    far_out = zsend(remote.at[0], fout_ref.at[zh], 9, (after, mate))

    for copy in (dg_own, ug_own, row_own):
        copy.wait()
    for copy in (dg_out, ug_out, row_out, near_out, far_out, fin):
        copy.wait()
    wu_in.wait_send()
    wd_in.wait_send()
    gathered_out(B)
    for s in (G, F):
        for h in (0, 1):
            for k in range(8):
                scatters[s, h, k].wait_send()

    def done(n, carry):
        pre_copy(n // 4, n % 4).wait_send()
        return carry

    lax.fori_loop(0, 12, done, 0)


def relay(pb, pg, pf, upper, lower, rows):
    hbm = pl.BlockSpec(memory_space=pl.ANY)
    shapes = [
        jax.ShapeDtypeStruct(rows.shape, BF16),
        jax.ShapeDtypeStruct((2, SLOTS, HALF), BF16),
        jax.ShapeDtypeStruct((2, SLOTS, HALF), BF16),
        jax.ShapeDtypeStruct(upper.shape, BF16),
        jax.ShapeDtypeStruct(lower.shape, BF16),
    ]
    dma = pltpu.SemaphoreType.DMA
    return pl.pallas_call(
        kernel,
        out_shape=shapes,
        in_specs=[hbm] * 6,
        out_specs=[hbm] * 5,
        scratch_shapes=[
            pltpu.VMEM((3, 4, 4, BLOCK, HALF), BF16),
            pltpu.VMEM((2, HALF, UNITS), BF16),
            pltpu.VMEM((2, UNITS, HALF), BF16),
            pltpu.VMEM((3, SLOTS, HALF), BF16),
            pltpu.VMEM((3, SLOTS, HALF), BF16),
            pltpu.VMEM((3, 4, 4 * BLOCK, 2 * UNITS), BF16),
            pltpu.VMEM((3, 4, 4 * BLOCK, 2 * UNITS), BF16),
            pltpu.VMEM((2, UNITS, HALF), BF16),
            pltpu.VMEM((2, HALF, UNITS), BF16),
            pltpu.VMEM((2, 2, 2, 4, BLOCK, QUARTER), BF16),
            pltpu.VMEM((2, 2, 2, 4, BLOCK, COLS), BF16),
            pltpu.VMEM((2, 2, 2, BLOCK, QUARTER), BF16),
            pltpu.VMEM((2, 2, 2, BLOCK, COLS), BF16),
            dma((3, 2, 8)),
            dma((3, 2, 8)),
            dma((2, 2, 8)),
            dma((2, 2, 8)),
            dma((3, 4)),
            dma((3, 4)),
            dma((11,)),
            dma((11,)),
            dma((8,)),
        ],
        compiler_params=pltpu.CompilerParams(
            collective_id=0, has_side_effects=True, vmem_limit_bytes=64 * 1024 * 1024
        ),
        cost_estimate=pl.CostEstimate(
            flops=28_000_000_000, bytes_accessed=40_000_000, transcendentals=2_000_000
        ),
        name="relay",
    )(pb, pg, pf, upper, lower, rows)


def from_behind(value, axis, steps):
    count = lax.axis_size(axis)
    pairs = [(source, (source + steps) % count) for source in range(count)]
    return lax.ppermute(value, axis, pairs)


def routing_plan(route_ids, route_weights, expert):
    matches = route_ids == expert
    active = jnp.any(matches, axis=-1)
    chosen = jnp.sum(jnp.where(matches, route_weights, jnp.float32(0.0)), axis=-1)
    ordinal = jnp.cumsum(active.astype(jnp.int32)) - 1
    places = jnp.arange(SLOTS, dtype=jnp.int32)
    hit = (ordinal[None, :] == places[:, None]) & active[None, :]
    return jnp.where(hit, 1.0, 0.0).astype(BF16), chosen


def pack_rows(selector, source):
    return jnp.dot(selector, source, preferred_element_type=F32).astype(BF16)


def unpack_rows(selector, packed):
    halves = [jnp.dot(selector.T, packed[h], preferred_element_type=F32) for h in (0, 1)]
    return jnp.concatenate(halves, axis=1)


def body(
    fwd_input,
    fwd_routes,
    fwd_weights,
    bwd_input,
    bwd_routes,
    bwd_weights,
    out_grad,
    up_weight,
    down_weight,
):
    expert = lax.axis_index("section")
    incoming = out_grad[0]
    select_b, weight_b = routing_plan(bwd_routes[0], bwd_weights[0], expert)
    packed_b = pack_rows(select_b, bwd_input[0])
    scaled_grad = (weight_b[:, None] * incoming.astype(F32)).astype(BF16)
    packed_g = pack_rows(select_b, scaled_grad)
    select_f, _ = routing_plan(fwd_routes[0], fwd_weights[0], expert)
    packed_f = pack_rows(select_f, fwd_input[0])
    routes_p = from_behind(fwd_routes[0], "section", 1)
    weights_p = from_behind(fwd_weights[0], "section", 1)
    rows_p, expert_p, rows_grad, up_grad, down_grad = relay(
        packed_b, packed_g, packed_f, up_weight[0], down_weight[0], fwd_input[0]
    )
    select_p, weight_p = routing_plan(routes_p, weights_p, (expert + 3) % 4)
    next_input = rows_p.astype(F32) + weight_p[:, None] * unpack_rows(select_p, expert_p)
    input_grad = incoming.astype(F32) + unpack_rows(select_b, rows_grad)
    return (
        next_input.astype(BF16)[None],
        input_grad.astype(BF16)[None],
        up_grad[None],
        down_grad[None],
    )


def solution(mesh):
    row_spec = P("section", "fsdp", None)
    in_specs = (row_spec,) * 7 + (P("section", None, "fsdp"), row_spec)
    out_specs = (row_spec, row_spec, P("section", None, "fsdp"), row_spec)
    return jax.shard_map(body, mesh=mesh, in_specs=in_specs, out_specs=out_specs, check_vma=False)
```

time: 1020 us -> 302 us (0.30)
  waiting for transfers between devices: 906 us -> 0.01 us
  Pallas kernels: 0 us -> 274 us
  matrix products: 86.9 us -> 7.79 us
  between operations: 13.9 us -> 0.8 us
    reduce_scatter x2 -> x0, waiting for transfers between devices: 483 us -> none  [the longest x1 246 us: body(): lax.psum_scatter(jnp.dot(block, lower, preferred_element_type=jnp.float32...]
    all_gather x3 -> x0, waiting for transfers between devices: 422 us -> none  [the longest x1 147 us: body(): lax.all_gather(packed_f, 'fsdp', axis=0, tiled=True)]
    pallas_call x0 -> x1, Pallas kernels: none -> 274 us  [relay(): pl.pallas_call(kernel, out_shape=shapes, in_specs=[hbm] * 6, out_specs=[h...]
    dot_general x12 -> x7, matrix products: 86.9 us -> 7.79 us  [the longest x3 5.1 us: pack_rows(): return jnp.dot(selector, source, preferred_element_type=F32).astype(BF16)]
  transfers between devices with their start and end apart: 6 -> 2, of which waited for: 5 -> 0; matrix products, arithmetic and copies ran while one was open for 8% -> 4% of each run, Pallas kernels for 0% -> 91%
where the time goes in v1:
time: 302 us; the launch traced here: 300 us
  Pallas kernels  274 us (91%)
  matrix products  7.79 us (3%)
  other arithmetic  7.43 us (2%)
  local copies, waits for them, and re-layouts  6.37 us (2%)
  starting transfers between devices  3.18 us (1%)
    pallas_call x1, Pallas kernels, relay(): pl.pallas_call(kernel, out_shape=shapes, in_specs=[hbm] * 6, out_specs=[h...  274 us
  transfers between devices with their start and end apart: 2, of which 0 were waited for; matrix products, arithmetic and copies ran while one was open for 4% of the time, Pallas kernels for 91%

profile of v1, /device:TPU:1, one launch (start us, length us, event | category | flops | bytes accessed | tf_op | source)
XLA Modules:
  0.0 299.7 jit_solution(14611133248816777129)
XLA Ops:
  0.6 0.0 copy-start.4
  0.6 3.1 %collective-permute-start.1 = (f32[128,2]{0,1:T(2,128)}, f32[128,2]{0,1:T(2,128)}, u32[]{:S(2)}, u32[]{:S(2)}) collective-permute-start(f32[128,2]{0,1:T(2,128)} %bitcast.50), channel_id=1, source_target_pairs={{0,32},{32,64},{64,96},{96,0},{1,33},{33,65},{65,97},{97,1},{2,34}... | collective-permute-start | bytes 3080 | tf_op jit(solution)/shard_map/ppermute | solution.py:525
  3.7 0.1 collective-permute-start
  3.8 0.7 compare_reduce_fusion
  4.6 0.7 fusion.65
  5.2 0.0 copy-start.10
  5.3 0.7 select_reduce_fusion.1
  6.0 0.1 copy.16
  6.1 0.2 reduce-window.24
  6.3 0.1 add_reduce_fusion.2
  6.4 0.0 copy-start.8
  6.4 0.1 copy.17
  6.5 0.2 reduce-window.25
  6.7 0.1 add_reduce_fusion.1
  6.8 2.6 convolution_convert_fusion.pf_ref
  9.4 0.0 copy-done.4
  9.4 0.0 copy-start
  9.4 1.2 convolution_convert_fusion.2.pb_ref
  10.5 0.0 copy-done.10
  10.5 0.0 copy-done.8
  10.5 0.4 copy-done
  11.0 1.3 convolution_convert_fusion.1.pg_ref
  12.3 274.1 %relay.1 = (bf16[128,6144]{1,0:T(8,128)(2,1)}, bf16[2,48,3072]{2,1,0:T(8,128)(2,1)}, bf16[2,48,3072]{2,1,0:T(8,128)(2,1)}, bf16[6144,256]{1,0:T(8,128)(2,1)}, bf16[256,6144]{1,0:T(8,128)(2,1)}) custom-call(bf16[48,6144]{1,0:T(8,128)(2,1)} %convolution_convert_fusion.2.pb_ref, bf16[48,6144]{1,0:T(8,128)(2,1)} %convolution_convert_fusion.1.pg_ref, ...), custom_call_target="tpu_custom_call" | custom-call | flops 28000000000 | bytes 40000000 | tf_op jit(solution)/shard_map/relay/pallas_call | solution.py:483
  286.4 0.0 copy-start.7
  286.4 0.0 copy-start.9
  286.4 0.0 copy-start.11
  286.5 0.0 copy-start.1
  286.5 1.5 convolution_bitcast_fusion
  288.0 0.0 copy-done.7
  288.0 0.0 copy-done.9
  288.0 0.0 copy-done.11
  288.0 0.4 convolution_bitcast_fusion.1
  288.4 0.0 copy-done.1
  288.4 0.0 copy-start.6
  288.4 1.5 fusion.2
  289.9 0.0 collective-permute-done
  289.9 0.7 fusion.66
  290.6 0.1 copy.18
  290.7 0.2 reduce-window.26
  290.9 0.1 add_reduce_fusion
  291.0 0.0 copy-done.6
  291.0 0.0 copy-start.5
  291.0 0.4 fusion.11
  291.4 0.4 fusion.13
  291.8 0.0 collective-permute-done.1
  291.8 0.7 select_reduce_fusion
  292.5 0.0 copy-done.5
  292.5 0.0 copy-start.3
  292.5 1.6 fusion.5
  294.1 0.8 copy-done.3
  295.0 0.0 copy-start.2
  295.0 1.7 copy.21
  296.6 1.4 copy-done.2
  298.0 1.7 copy.22
  (3 shorter events, 0.0 us)
Async XLA Ops:
  0.6 8.7 %copy-start.4 = (bf16[1,128,6144]{2,1,0:T(8,128)(2,1)S(1)}, bf16[1,128,6144]{2,1,0:T(8,128)(2,1)}, u32[]{:S(2)}) copy-start(bf16[1,128,6144]{2,1,0:T(8,128)(2,1)} %param.12) | copy-start | bytes 4718596
  0.6 291.2 %collective-permute-start.1 = (f32[128,2]{0,1:T(2,128)}, f32[128,2]{0,1:T(2,128)}, u32[]{:S(2)}, u32[]{:S(2)}) collective-permute-start(f32[128,2]{0,1:T(2,128)} %bitcast.50), channel_id=1, source_target_pairs={{0,32},{32,64},{64,96},{96,0},{1,33},{33,65},{65,97},{97,1},{2,34}... | collective-permute-start | bytes 3080 | tf_op jit(solution)/shard_map/ppermute | solution.py:525
  3.7 286.2 %collective-permute-start = (s32[128,2]{0,1:T(2,128)}, s32[128,2]{0,1:T(2,128)}, u32[]{:S(2)}, u32[]{:S(2)}) collective-permute-start(s32[128,2]{0,1:T(2,128)} %bitcast.47), channel_id=1, source_target_pairs={{0,32},{32,64},{64,96},{96,0},{1,33},{33,65},{65,97},{97,1},{2,34}... | collective-permute-start | bytes 3080 | tf_op jit(solution)/shard_map/ppermute | solution.py:525
  5.2 5.3 %copy-start.10 = (pred[128]{0:T(512)(128)(4,1)}, pred[128]{0:T(512)(128)(4,1)S(1)}, u32[]{:S(2)}) copy-start(pred[128]{0:T(512)(128)(4,1)S(1)} %fusion.65) | copy-start | bytes 388
  6.4 4.2 %copy-start.8 = (s32[128]{0:T(128)}, s32[128]{0:T(128)S(1)}, u32[]{:S(2)}) copy-start(s32[128]{0:T(128)S(1)} %add_reduce_fusion.2) | copy-start | bytes 1540
  9.4 1.6 copy-start
  286.4 1.6 copy-start.7
  286.4 1.6 copy-start.9
  286.4 1.6 copy-start.11
  286.5 2.0 copy-start.1
  288.4 2.6 copy-start.6
  291.0 1.5 copy-start.5
  292.5 2.5 copy-start.3
  295.0 3.0 %copy-start.2 = (bf16[256,6144]{1,0:T(8,128)(2,1)S(1)}, bf16[256,6144]{1,0:T(8,128)(2,1)}, u32[]{:S(2)}) copy-start(bf16[256,6144]{1,0:T(8,128)(2,1)} %get-tuple-element.13) | copy-start | bytes 9437188

commit v2 on v1

--- a/solution.py
+++ b/solution.py
@@ -16,6 +16,7 @@
 D = 6144
 HALF = D // 2
 UNITS = 256
+TOKENS = 128
 BLOCK = 2 * CAP
 COLS = HALF // 2
 QUARTER = COLS // 2
@@ -24,18 +25,33 @@
 B, G, F = 0, 1, 2
 
 
+def route(plan_ref, base, expert):
+    hit = [plan_ref[pl.ds(base + k, 1), :] == expert for k in (0, 1)]
+    share = [plan_ref[pl.ds(base + 2 + k, 1), :] for k in (0, 1)]
+    active = jnp.where(hit[0] | hit[1], 1.0, 0.0)
+    weight = jnp.where(hit[0], share[0], 0.0) + jnp.where(hit[1], share[1], 0.0)
+    earlier = lax.broadcasted_iota(jnp.int32, (TOKENS, TOKENS), 0)
+    later = lax.broadcasted_iota(jnp.int32, (TOKENS, TOKENS), 1)
+    before = jnp.where(earlier < later, 1.0, 0.0).astype(BF16)
+    spread = jnp.broadcast_to(active, (8, TOKENS)).astype(BF16)
+    order = jnp.dot(spread, before, preferred_element_type=F32)[0:1]
+    return order, active, weight
+
+
 def kernel(
-    pb_ref,
-    pg_ref,
-    pf_ref,
+    plan_ref,
+    xb_ref,
+    xg_ref,
+    xf_ref,
     up_ref,
     down_ref,
-    xf_ref,
     fin_ref,
     fout_ref,
     rout_ref,
     ug_ref,
     dg_ref,
+    info_ref,
+    info,
     rows,
     wu,
     wd,
@@ -113,12 +129,33 @@
     def zsend(src, dst, index, device=pair):
         return send(src, dst, z_send.at[index], z_recv.at[index], device)
 
-    packed = (pb_ref, pg_ref, pf_ref)
-    token = [zsend(packed[s].at[:, other], remote.at[s], s) for s in (B, G, F)]
-    own = [keep(packed[s].at[:, mine], local.at[s], s) for s in (B, G, F)]
-    wu_in = zsend(up_ref.at[other], wu.at[1], 3)
-    wu_own = keep(up_ref.at[mine], wu.at[0], 3)
-    wd_own = keep(down_ref.at[:, mine], wd.at[0], 4)
+    def up_part(n):
+        width = HALF // 4
+        start = pl.multiple_of((1 - zh) * HALF + n * width, width)
+        return zsend(up_ref.at[pl.ds(start, width)], wu.at[1, pl.ds(n * width, width)], 11 + n)
+
+    wu_in = [up_part(0)]
+    upper, lower = pl.ds(0, TOKENS), pl.ds(TOKENS, TOKENS)
+
+    def fetch(source, where, index):
+        return [
+            keep(source.at[:, pl.ds(half * HALF, HALF)], dgs.at[half, where], index + half)
+            for half in (0, 1)
+        ]
+
+    fetched = {B: fetch(xb_ref, upper, 0), G: fetch(xg_ref, lower, 2)}
+
+    def selector(order, active, count, offset):
+        place = lax.broadcasted_iota(jnp.int32, (count, TOKENS), 0).astype(F32)
+        return jnp.where((order + offset == place) & (active > 0.0), 1.0, 0.0)
+
+    expert = sec.astype(F32)
+    order_b, active_b, weight_b = route(plan_ref, 4, expert)
+    order_f, active_f, weight_f = route(plan_ref, 0, expert)
+    shift = (CAP * zh).astype(F32)
+    line = lax.broadcasted_iota(jnp.int32, (8, TOKENS), 0)
+    slots_f = jnp.where(active_f > 0.0, order_f, -1.0)
+    info[...] = jnp.where(line == 0, slots_f, jnp.where(line == 1, weight_f, 0.0))
 
     slot = lax.broadcasted_iota(jnp.int32, (BLOCK, SLOTS), 1)
     row = lax.broadcasted_iota(jnp.int32, (BLOCK, SLOTS), 0)
@@ -129,13 +166,36 @@
 
     place_mine, place_other = place(zh), place(1 - zh)
 
+    def pack(s, where, order, active, weight):
+        for copy in fetched[s]:
+            copy.wait()
+        small = selector(order, active, SLOTS, 0.0)
+        wide = selector(order, active, BLOCK, shift)
+        small_w = jnp.sum(small * weight, axis=1, keepdims=True)
+        wide_w = jnp.sum(wide * weight, axis=1, keepdims=True)
+        for c in range(0, HALF, TILE):
+            cols = pl.ds(c, TILE)
+            value = jnp.dot(small.astype(BF16), dgs[1 - zh, where, cols], preferred_element_type=F32)
+            if s == G:
+                value = value * small_w
+            local[s, :, cols] = value.astype(BF16)
+        copy = zsend(local.at[s], remote.at[s], s)
+        for c in range(0, HALF, TILE):
+            cols = pl.ds(c, TILE)
+            value = jnp.dot(wide.astype(BF16), dgs[zh, where, cols], preferred_element_type=F32)
+            if s == G:
+                value = value * wide_w
+            rows[s, mx, my, :, cols] = value.astype(BF16)
+        return copy
+
+    token = {}
+
     def fill(s):
         token[s].wait_recv()
-        own[s].wait()
         for c in range(0, HALF, TILE):
             cols = pl.ds(c, TILE)
-            total = jnp.dot(place_mine, local[s, :, cols], preferred_element_type=F32)
-            total += jnp.dot(place_other, remote[s, :, cols], preferred_element_type=F32)
+            total = jnp.dot(place_other, remote[s, :, cols], preferred_element_type=F32)
+            total += rows[s, mx, my, :, cols].astype(F32)
             rows[s, mx, my, :, cols] = total.astype(BF16)
 
     def up4(i):
@@ -394,6 +454,15 @@
                 place_other, block, lead, preferred_element_type=F32
             ).astype(BF16)
 
+    token[B] = pack(B, upper, order_b, active_b, weight_b)
+    fetched[F] = fetch(xf_ref, upper, 0)
+    token[G] = pack(G, lower, order_b, active_b, weight_b)
+    wu_in.append(up_part(1))
+    wu_own = keep(up_ref.at[mine], wu.at[0], 4)
+    wd_own = keep(down_ref.at[:, mine], wd.at[0], 5)
+    token[F] = pack(F, upper, order_f, active_f, weight_f)
+    wu_in.append(up_part(2))
+    wu_in.append(up_part(3))
     fill(B)
     gather1(B)
     gather2(B)
@@ -407,13 +476,15 @@
     fill(F)
     gather1(F)
     gather5(B)
-    wu_in.wait_recv()
+    for copy in wu_in:
+        copy.wait_recv()
     wu_own.wait()
     partial_up(B)
     gather4(G)
     gather2(F)
     gather3(F)
     fin = zsend(xf_ref, fin_ref, 10, (after, me))
+    told = zsend(info, info_ref, 3, (after, me))
     gather5(G)
     wd_in.wait_recv()
     wd_own.wait()
@@ -424,13 +495,13 @@
     activate_back()
     down_grad()
     dg_out = zsend(dgs.at[1], dg_ref.at[:, mine], 5)
-    dg_own = keep(dgs.at[0], dg_ref.at[:, mine], 5)
+    dg_own = keep(dgs.at[0], dg_ref.at[:, mine], 6)
     gathered_out(G)
     rows_out(G, G, wu, last)
     scatter1(G)
     up_grad()
     ug_out = zsend(ugs.at[1], ug_ref.at[mine], 6)
-    ug_own = keep(ugs.at[0], ug_ref.at[mine], 6)
+    ug_own = keep(ugs.at[0], ug_ref.at[mine], 7)
     scatter2(G)
     activate_fwd()
     gathered_out(F)
@@ -444,7 +515,7 @@
     token[G].wait_send()
     token[F].wait_send()
     scatter5(G, local.at[0], local.at[1])
-    row_own = keep(local.at[0], rout_ref.at[zh], 7)
+    row_own = keep(local.at[0], rout_ref.at[zh], 8)
     row_out = zsend(local.at[1], rout_ref.at[zh], 7)
     scatter4(F)
     scatter5(F, local.at[2], remote.at[0])
@@ -453,9 +524,10 @@
 
     for copy in (dg_own, ug_own, row_own):
         copy.wait()
-    for copy in (dg_out, ug_out, row_out, near_out, far_out, fin):
+    for copy in (dg_out, ug_out, row_out, near_out, far_out, fin, told):
         copy.wait()
-    wu_in.wait_send()
+    for copy in wu_in:
+        copy.wait_send()
     wd_in.wait_send()
     gathered_out(B)
     for s in (G, F):
@@ -470,22 +542,24 @@
     lax.fori_loop(0, 12, done, 0)
 
 
-def relay(pb, pg, pf, upper, lower, rows):
+def relay(plan, xb, xg, xf, upper, lower):
     hbm = pl.BlockSpec(memory_space=pl.ANY)
     shapes = [
-        jax.ShapeDtypeStruct(rows.shape, BF16),
+        jax.ShapeDtypeStruct(xf.shape, BF16),
         jax.ShapeDtypeStruct((2, SLOTS, HALF), BF16),
         jax.ShapeDtypeStruct((2, SLOTS, HALF), BF16),
         jax.ShapeDtypeStruct(upper.shape, BF16),
         jax.ShapeDtypeStruct(lower.shape, BF16),
+        jax.ShapeDtypeStruct((8, TOKENS), F32),
     ]
     dma = pltpu.SemaphoreType.DMA
     return pl.pallas_call(
         kernel,
         out_shape=shapes,
-        in_specs=[hbm] * 6,
-        out_specs=[hbm] * 5,
+        in_specs=[pl.BlockSpec(memory_space=pltpu.VMEM)] + [hbm] * 5,
+        out_specs=[hbm] * 6,
         scratch_shapes=[
+            pltpu.VMEM((8, TOKENS), F32),
             pltpu.VMEM((3, 4, 4, BLOCK, HALF), BF16),
             pltpu.VMEM((2, HALF, UNITS), BF16),
             pltpu.VMEM((2, UNITS, HALF), BF16),
@@ -505,9 +579,9 @@
             dma((2, 2, 8)),
             dma((3, 4)),
             dma((3, 4)),
-            dma((11,)),
-            dma((11,)),
-            dma((8,)),
+            dma((15,)),
+            dma((15,)),
+            dma((9,)),
         ],
         compiler_params=pltpu.CompilerParams(
             collective_id=0, has_side_effects=True, vmem_limit_bytes=64 * 1024 * 1024
@@ -516,32 +590,57 @@
             flops=28_000_000_000, bytes_accessed=40_000_000, transcendentals=2_000_000
         ),
         name="relay",
-    )(pb, pg, pf, upper, lower, rows)
-
-
-def from_behind(value, axis, steps):
-    count = lax.axis_size(axis)
-    pairs = [(source, (source + steps) % count) for source in range(count)]
-    return lax.ppermute(value, axis, pairs)
-
-
-def routing_plan(route_ids, route_weights, expert):
-    matches = route_ids == expert
-    active = jnp.any(matches, axis=-1)
-    chosen = jnp.sum(jnp.where(matches, route_weights, jnp.float32(0.0)), axis=-1)
-    ordinal = jnp.cumsum(active.astype(jnp.int32)) - 1
-    places = jnp.arange(SLOTS, dtype=jnp.int32)
-    hit = (ordinal[None, :] == places[:, None]) & active[None, :]
-    return jnp.where(hit, 1.0, 0.0).astype(BF16), chosen
-
-
-def pack_rows(selector, source):
-    return jnp.dot(selector, source, preferred_element_type=F32).astype(BF16)
-
-
-def unpack_rows(selector, packed):
-    halves = [jnp.dot(selector.T, packed[h], preferred_element_type=F32) for h in (0, 1)]
-    return jnp.concatenate(halves, axis=1)
+    )(plan, xb, xg, xf, upper, lower)
+
+
+def column(line):
+    down = lax.broadcasted_iota(jnp.int32, (TOKENS, TOKENS), 0)
+    across = lax.broadcasted_iota(jnp.int32, (TOKENS, TOKENS), 1)
+    return jnp.sum(jnp.where(down == across, line, 0.0), axis=1, keepdims=True)
+
+
+def finish_kernel(
+    plan_ref, info_ref, xg_ref, fin_ref, fout_ref, rout_ref, ug_ref, dg_ref, next_ref, grad_ref, up_ref, down_ref, sem
+):
+    copies = [
+        pltpu.make_async_copy(ug_ref, up_ref, sem.at[0]),
+        pltpu.make_async_copy(dg_ref, down_ref, sem.at[1]),
+    ]
+    for copy in copies:
+        copy.start()
+    expert = lax.axis_index("section").astype(F32)
+    order, active, _ = route(plan_ref, 4, expert)
+    lead = (((0,), (0,)), ((), ()))
+    place = lax.broadcasted_iota(jnp.int32, (SLOTS, TOKENS), 0).astype(F32)
+    mine = jnp.where((order == place) & (active > 0.0), 1.0, 0.0).astype(BF16)
+    theirs = jnp.where(info_ref[0:1, :] == place, 1.0, 0.0).astype(BF16)
+    weight = column(info_ref[1:2, :])
+    for half in (0, 1):
+        for c in range(0, HALF, TILE):
+            here, there = pl.ds(c, TILE), pl.ds(half * HALF + c, TILE)
+            spread = lax.dot_general(theirs, fout_ref[half, :, here], lead, preferred_element_type=F32)
+            next_ref[:, there] = (fin_ref[:, there].astype(F32) + weight * spread).astype(BF16)
+            spread = lax.dot_general(mine, rout_ref[half, :, here], lead, preferred_element_type=F32)
+            grad_ref[:, there] = (xg_ref[:, there].astype(F32) + spread).astype(BF16)
+    for copy in copies:
+        copy.wait()
+
+
+def finish(plan, info, xg, fin, fout, rout, up_grad, down_grad):
+    hbm = pl.BlockSpec(memory_space=pl.ANY)
+    vmem = pl.BlockSpec(memory_space=pltpu.VMEM)
+    return pl.pallas_call(
+        finish_kernel,
+        out_shape=[jax.ShapeDtypeStruct(a.shape, BF16) for a in (fin, xg, up_grad, down_grad)],
+        in_specs=[vmem] * 6 + [hbm] * 2,
+        out_specs=[vmem] * 2 + [hbm] * 2,
+        scratch_shapes=[pltpu.SemaphoreType.DMA((2,))],
+        compiler_params=pltpu.CompilerParams(vmem_limit_bytes=64 * 1024 * 1024),
+        cost_estimate=pl.CostEstimate(
+            flops=150_000_000, bytes_accessed=20_000_000, transcendentals=0
+        ),
+        name="finish",
+    )(plan, info, xg, fin, fout, rout, up_grad, down_grad)
 
 
 def body(
@@ -555,28 +654,13 @@
     up_weight,
     down_weight,
 ):
-    expert = lax.axis_index("section")
-    incoming = out_grad[0]
-    select_b, weight_b = routing_plan(bwd_routes[0], bwd_weights[0], expert)
-    packed_b = pack_rows(select_b, bwd_input[0])
-    scaled_grad = (weight_b[:, None] * incoming.astype(F32)).astype(BF16)
-    packed_g = pack_rows(select_b, scaled_grad)
-    select_f, _ = routing_plan(fwd_routes[0], fwd_weights[0], expert)
-    packed_f = pack_rows(select_f, fwd_input[0])
-    routes_p = from_behind(fwd_routes[0], "section", 1)
-    weights_p = from_behind(fwd_weights[0], "section", 1)
-    rows_p, expert_p, rows_grad, up_grad, down_grad = relay(
-        packed_b, packed_g, packed_f, up_weight[0], down_weight[0], fwd_input[0]
+    lines = [fwd_routes[0].T, fwd_weights[0].T, bwd_routes[0].T, bwd_weights[0].T]
+    plan = jnp.concatenate([line.astype(F32) for line in lines], axis=0)
+    fin, fout, rout, up_grad, down_grad, info = relay(
+        plan, bwd_input[0], out_grad[0], fwd_input[0], up_weight[0], down_weight[0]
     )
-    select_p, weight_p = routing_plan(routes_p, weights_p, (expert + 3) % 4)
-    next_input = rows_p.astype(F32) + weight_p[:, None] * unpack_rows(select_p, expert_p)
-    input_grad = incoming.astype(F32) + unpack_rows(select_b, rows_grad)
-    return (
-        next_input.astype(BF16)[None],
-        input_grad.astype(BF16)[None],
-        up_grad[None],
-        down_grad[None],
-    )
+    outs = finish(plan, info, out_grad[0], fin, fout, rout, up_grad, down_grad)
+    return tuple(out[None] for out in outs)
 
 
 def solution(mesh):

time: 302 us -> 477 us (1.58)
  Pallas kernels: 274 us -> 472 us
  matrix products: 7.79 us -> 0 us
  local copies, waits for them, and re-layouts: 6.37 us -> 0 us
  other arithmetic: 7.43 us -> 1.99 us
    pallas_call x1 -> x2, Pallas kernels: 274 us -> 472 us  [the longest x1 277 us: relay(): pl.pallas_call(kernel, out_shape=shapes, in_specs=[pl.BlockSpec(memory_sp...]
    dot_general x7 -> x0, matrix products: 7.79 us -> none  [the longest x3 5.1 us: pack_rows(): return jnp.dot(selector, source, preferred_element_type=F32).astype(BF16)]
    unnamed x26 -> x0, local copies, waits for them, and re-layouts: 6.03 us -> none
  transfers between devices with their start and end apart: 2 -> 0, of which waited for: 0 -> 0; matrix products, arithmetic and copies ran while one was open for 4% -> 0% of each run, Pallas kernels for 91% -> 0%
where the time goes in v2:
time: 477 us; the launch traced here: 475 us
  Pallas kernels  472 us (99%)
    pallas_call x1, Pallas kernels, relay(): pl.pallas_call(kernel, out_shape=shapes, in_specs=[pl.BlockSpec(memory_sp...  277 us
    pallas_call x1, Pallas kernels, finish(): pl.pallas_call(finish_kernel, out_shape=[jax.ShapeDtypeStruct(a.shape, BF...  196 us

profile of v2, /device:TPU:1, one launch (start us, length us, event | category | flops | bytes accessed | tf_op | source)
XLA Modules:
  0.0 474.9 jit_solution(3843449664080593231)
XLA Ops:
  0.6 0.7 convert_bitcast_fusion
  1.3 1.3 pad_maximum_fusion.plan_ref
  2.6 276.7 %relay.1 = (bf16[128,6144]{1,0:T(8,128)(2,1)}, bf16[2,48,3072]{2,1,0:T(8,128)(2,1)}, bf16[2,48,3072]{2,1,0:T(8,128)(2,1)}, bf16[6144,256]{1,0:T(8,128)(2,1)}, bf...) custom-call(f32[8,128]{1,0:T(8,128)} %pad_maximum_fusion.plan_ref, bf16[128,6144]{1,0:T(8,128)(2,1)} %bitcast.31, ...), custom_call_target="tpu_custom_call" | custom-call | flops 28000000000 | bytes 40000000 | tf_op jit(solution)/shard_map/relay/pallas_call | solution.py:556
  279.3 195.6 %finish.1 = (bf16[128,6144]{1,0:T(8,128)(2,1)}, bf16[128,6144]{1,0:T(8,128)(2,1)}, bf16[6144,256]{1,0:T(8,128)(2,1)}, bf16[256,6144]{1,0:T(8,128)(2,1)}) custom-call(f32[8,128]{1,0:T(8,128)} %pad_maximum_fusion.plan_ref, f32[8,128]{1,0:T(8,128)} %get-tuple-element.14.info_ref, bf16[128,6144]{1,0:T(8,128)(2,1)} %bitcast.24, ...), custom_call_target="tpu_custom_call" | custom-call | flops 150000000 | bytes 20000000 | tf_op jit(solution)/shard_map/finish/pallas_call | solution.py:632

commit v3 on v2

--- a/solution.py
+++ b/solution.py
@@ -22,7 +22,9 @@
 QUARTER = COLS // 2
 TILE = 768
 
-B, G, F = 0, 1, 2
+EXTRA = 1536
+KEPT = HALF - EXTRA
+B, G, F, X = 0, 1, 2, 3
 
 
 def route(plan_ref, base, expert):
@@ -53,6 +55,9 @@
     info_ref,
     info,
     rows,
+    extra,
+    sent,
+    got,
     wu,
     wd,
     local,
@@ -143,7 +148,9 @@
             for half in (0, 1)
         ]
 
-    fetched = {B: fetch(xb_ref, upper, 0), G: fetch(xg_ref, lower, 2)}
+    fetched = {F: fetch(xf_ref, upper, 0), B: fetch(xb_ref, lower, 2)}
+
+    token = {}
 
     def selector(order, active, count, offset):
         place = lax.broadcasted_iota(jnp.int32, (count, TOKENS), 0).astype(F32)
@@ -180,6 +187,13 @@
                 value = value * small_w
             local[s, :, cols] = value.astype(BF16)
         copy = zsend(local.at[s], remote.at[s], s)
+        if s == G:
+            for c in range(0, EXTRA, TILE):
+                value = jnp.dot(
+                    small.astype(BF16), dgs[zh, where, pl.ds(KEPT + c, TILE)], preferred_element_type=F32
+                )
+                sent[:, pl.ds(c, TILE)] = (value * small_w).astype(BF16)
+            token[X] = zsend(sent, got, 15)
         for c in range(0, HALF, TILE):
             cols = pl.ds(c, TILE)
             value = jnp.dot(wide.astype(BF16), dgs[zh, where, cols], preferred_element_type=F32)
@@ -188,7 +202,15 @@
             rows[s, mx, my, :, cols] = value.astype(BF16)
         return copy
 
-    token = {}
+    def fill_extra():
+        token[X].wait_recv()
+        for c in range(0, EXTRA, TILE):
+            cols = pl.ds(c, TILE)
+            total = jnp.dot(place_other, got[:, cols], preferred_element_type=F32)
+            total += jnp.dot(
+                place_mine, local[G, :, pl.ds(KEPT + c, TILE)], preferred_element_type=F32
+            )
+            extra[mx, my, :, cols] = total.astype(BF16)
 
     def fill(s):
         token[s].wait_recv()
@@ -204,12 +226,19 @@
     def one(h, i):
         return (up4(i), my) if h == 0 else (mx, up4(i))
 
+    def span(s):
+        return EXTRA // 2 if s == X else COLS
+
     def g1(s, h, i, start, width):
         x, y = one(h, i)
+        if s == X:
+            return extra.at[x, y, :, pl.ds(h * span(s) + start, width)]
         return rows.at[s, x, y, :, pl.ds(h * COLS + start, width)]
 
     def g4(s, h, j, start, width):
-        cols = pl.ds(h * COLS + start, width)
+        cols = pl.ds(h * span(s) + start, width)
+        if s == X:
+            return extra.at[:, up4(j), :, cols] if h == 0 else extra.at[up4(j), :, :, cols]
         if h == 0:
             return rows.at[s, :, up4(j), :, cols]
         return rows.at[s, up4(j), :, :, cols]
@@ -229,31 +258,31 @@
 
     def gather1(s):
         for h in (0, 1):
-            ref = g1(s, h, first[h], 0, COLS)
+            ref = g1(s, h, first[h], 0, span(s))
             gsend(s, h, 0, ref, dev1(h, 1))
             gsend(s, h, 1, ref, dev1(h, -1))
 
     def gather2(s):
         for h in (0, 1):
             gathers[s, h, 0].wait_recv()
-            gsend(s, h, 2, g1(s, h, first[h] - 1, 0, QUARTER), dev1(h, 1))
+            gsend(s, h, 2, g1(s, h, first[h] - 1, 0, span(s) // 2), dev1(h, 1))
             gathers[s, h, 1].wait_recv()
-            gsend(s, h, 3, g1(s, h, first[h] + 1, QUARTER, QUARTER), dev1(h, -1))
+            gsend(s, h, 3, g1(s, h, first[h] + 1, span(s) // 2, span(s) // 2), dev1(h, -1))
 
     def gather3(s):
         for h in (0, 1):
             gathers[s, h, 2].wait_recv()
             gathers[s, h, 3].wait_recv()
-            ref = g4(s, h, second[h], 0, COLS)
+            ref = g4(s, h, second[h], 0, span(s))
             gsend(s, h, 4, ref, dev2(h, 1))
             gsend(s, h, 5, ref, dev2(h, -1))
 
     def gather4(s):
         for h in (0, 1):
             gathers[s, h, 4].wait_recv()
-            gsend(s, h, 6, g4(s, h, second[h] - 1, 0, QUARTER), dev2(h, 1))
+            gsend(s, h, 6, g4(s, h, second[h] - 1, 0, span(s) // 2), dev2(h, 1))
             gathers[s, h, 5].wait_recv()
-            gsend(s, h, 7, g4(s, h, second[h] + 1, QUARTER, QUARTER), dev2(h, -1))
+            gsend(s, h, 7, g4(s, h, second[h] + 1, span(s) // 2, span(s) // 2), dev2(h, -1))
 
     def gather5(s):
         for h in (0, 1):
@@ -310,17 +339,29 @@
     def activate_back():
         def step(i, carry):
             pre_copy(B, i).wait_recv()
-            pre_copy(G, i).wait_recv()
+            pre_copy(B, i).wait_send()
             hidden, slope = [], []
             for u in (0, 1):
                 pre = whole(B, i, u)
                 gate = sigmoid(pre)
                 hidden.append((pre * gate).astype(BF16))
-                back = whole(G, i, u)
-                slope.append((back * (gate * (1.0 + pre * (1.0 - gate)))).astype(BF16))
+                slope.append((gate * (1.0 + pre * (1.0 - gate))).astype(BF16))
             for u in (0, 1):
                 peer[B, i, :, pl.ds(u * UNITS, UNITS)] = hidden[u]
-                peer[G, i, :, pl.ds(u * UNITS, UNITS)] = slope[u]
+                part[B, i, :, pl.ds(u * UNITS, UNITS)] = slope[u]
+            return carry
+
+        lax.fori_loop(0, 4, step, 0)
+
+    def back_grad():
+        def step(i, carry):
+            pre_copy(G, i).wait_recv()
+            value = []
+            for u in (0, 1):
+                slope = part[B, i, :, pl.ds(u * UNITS, UNITS)].astype(F32)
+                value.append((whole(G, i, u) * slope).astype(BF16))
+            for u in (0, 1):
+                peer[G, i, :, pl.ds(u * UNITS, UNITS)] = value[u]
             return carry
 
         lax.fori_loop(0, 4, step, 0)
@@ -339,7 +380,7 @@
         lax.fori_loop(0, 4, step, 0)
 
     def down_grad():
-        for u in (1, 0):
+        for u, width in ((1, KEPT), (0, HALF)):
             def step(c, carry):
                 cols = pl.ds(pl.multiple_of(c * TILE, TILE), TILE)
                 left = peer[B, :, :, pl.ds(u * UNITS, UNITS)].reshape(16 * BLOCK, UNITS)
@@ -348,7 +389,18 @@
                 dgs[u, :, cols] = value.astype(BF16)
                 return carry
 
-            lax.fori_loop(0, HALF // TILE, step, 0)
+            lax.fori_loop(0, width // TILE, step, 0)
+
+    def down_grad_extra():
+        def step(c, carry):
+            start = pl.multiple_of(c * TILE, TILE)
+            left = peer[B, :, :, pl.ds(0, UNITS)].reshape(16 * BLOCK, UNITS)
+            right = extra[:, :, :, pl.ds(start, TILE)].reshape(16 * BLOCK, TILE)
+            value = lax.dot_general(left, right, lead, preferred_element_type=F32)
+            dgs[1, :, pl.ds(KEPT + start, TILE)] = value.astype(BF16)
+            return carry
+
+        lax.fori_loop(0, EXTRA // TILE, step, 0)
 
     def up_grad():
         def step(c, carry):
@@ -454,75 +506,87 @@
                 place_other, block, lead, preferred_element_type=F32
             ).astype(BF16)
 
-    token[B] = pack(B, upper, order_b, active_b, weight_b)
-    fetched[F] = fetch(xf_ref, upper, 0)
-    token[G] = pack(G, lower, order_b, active_b, weight_b)
+    token[F] = pack(F, upper, order_f, active_f, weight_f)
+    fetched[G] = fetch(xg_ref, upper, 0)
+    token[B] = pack(B, lower, order_b, active_b, weight_b)
     wu_in.append(up_part(1))
     wu_own = keep(up_ref.at[mine], wu.at[0], 4)
     wd_own = keep(down_ref.at[:, mine], wd.at[0], 5)
-    token[F] = pack(F, upper, order_f, active_f, weight_f)
+    token[G] = pack(G, upper, order_b, active_b, weight_b)
     wu_in.append(up_part(2))
     wu_in.append(up_part(3))
+    fill(F)
+    gather1(F)
+    gather2(F)
+    gather3(F)
+    wd_in = zsend(down_ref.at[:, other], wd.at[1], 4)
     fill(B)
     gather1(B)
     gather2(B)
+    gather4(F)
     gather3(B)
-    wd_in = zsend(down_ref.at[:, other], wd.at[1], 4)
     fill(G)
     gather1(G)
-    gather2(G)
-    gather4(B)
-    gather3(G)
-    fill(F)
-    gather1(F)
-    gather5(B)
+    gather5(F)
+    fill_extra()
     for copy in wu_in:
         copy.wait_recv()
     wu_own.wait()
+    partial_up(F)
+    gather4(B)
+    gather2(G)
+    gather3(G)
+    gather5(B)
     partial_up(B)
     gather4(G)
-    gather2(F)
-    gather3(F)
+    gather1(X)
+    gather2(X)
+    gather3(X)
+    activate_fwd()
+    gathered_out(F)
+    wd_in.wait_recv()
+    wd_own.wait()
+    rows_out(F, F, wd, None)
+    scatter1(F)
+    gather5(G)
+    partial_back(G)
+    scatter2(F)
+    activate_back()
+    gather4(X)
+    down_grad()
+    kept = pl.ds(pl.multiple_of(zh * HALF, HALF), KEPT)
+    dg_out = zsend(dgs.at[1, :, pl.ds(0, KEPT)], dg_ref.at[:, kept], 5)
+    dg_own = keep(dgs.at[0], dg_ref.at[:, mine], 6)
+    gathered_out(G)
+    scatter3(F)
     fin = zsend(xf_ref, fin_ref, 10, (after, me))
     told = zsend(info, info_ref, 3, (after, me))
-    gather5(G)
-    wd_in.wait_recv()
-    wd_own.wait()
-    partial_back(G)
-    gather4(F)
-    gather5(F)
-    partial_up(F)
-    activate_back()
-    down_grad()
-    dg_out = zsend(dgs.at[1], dg_ref.at[:, mine], 5)
-    dg_own = keep(dgs.at[0], dg_ref.at[:, mine], 6)
-    gathered_out(G)
+    back_grad()
     rows_out(G, G, wu, last)
     scatter1(G)
     up_grad()
     ug_out = zsend(ugs.at[1], ug_ref.at[mine], 6)
     ug_own = keep(ugs.at[0], ug_ref.at[mine], 7)
+    gather5(X)
+    down_grad_extra()
+    far = pl.ds(pl.multiple_of((1 - zh) * HALF + KEPT, EXTRA), EXTRA)
+    dg_far = keep(dgs.at[1, :, pl.ds(KEPT, EXTRA)], dg_ref.at[:, far], 9)
+    scatter4(F)
     scatter2(G)
-    activate_fwd()
-    gathered_out(F)
-    rows_out(F, F, wd, None)
-    scatter1(F)
-    scatter3(G)
-    scatter2(F)
-    scatter4(G)
-    scatter3(F)
     token[B].wait_send()
     token[G].wait_send()
     token[F].wait_send()
+    token[X].wait_send()
+    scatter5(F, local.at[2], remote.at[0])
+    near_out = zsend(local.at[2], fout_ref.at[zh], 8, (after, me))
+    far_out = zsend(remote.at[0], fout_ref.at[zh], 9, (after, mate))
+    scatter3(G)
+    scatter4(G)
     scatter5(G, local.at[0], local.at[1])
     row_own = keep(local.at[0], rout_ref.at[zh], 8)
     row_out = zsend(local.at[1], rout_ref.at[zh], 7)
-    scatter4(F)
-    scatter5(F, local.at[2], remote.at[0])
-    near_out = zsend(local.at[2], fout_ref.at[zh], 8, (after, me))
-    far_out = zsend(remote.at[0], fout_ref.at[zh], 9, (after, mate))
-
-    for copy in (dg_own, ug_own, row_own):
+
+    for copy in (dg_own, dg_far, ug_own, row_own):
         copy.wait()
     for copy in (dg_out, ug_out, row_out, near_out, far_out, fin, told):
         copy.wait()
@@ -530,6 +594,7 @@
         copy.wait_send()
     wd_in.wait_send()
     gathered_out(B)
+    gathered_out(X)
     for s in (G, F):
         for h in (0, 1):
             for k in range(8):
@@ -539,7 +604,7 @@
         pre_copy(n // 4, n % 4).wait_send()
         return carry
 
-    lax.fori_loop(0, 12, done, 0)
+    lax.fori_loop(4, 12, done, 0)
 
 
 def relay(plan, xb, xg, xf, upper, lower):
@@ -561,6 +626,9 @@
         scratch_shapes=[
             pltpu.VMEM((8, TOKENS), F32),
             pltpu.VMEM((3, 4, 4, BLOCK, HALF), BF16),
+            pltpu.VMEM((4, 4, BLOCK, EXTRA), BF16),
+            pltpu.VMEM((SLOTS, EXTRA), BF16),
+            pltpu.VMEM((SLOTS, EXTRA), BF16),
             pltpu.VMEM((2, HALF, UNITS), BF16),
             pltpu.VMEM((2, UNITS, HALF), BF16),
             pltpu.VMEM((3, SLOTS, HALF), BF16),
@@ -573,15 +641,15 @@
             pltpu.VMEM((2, 2, 2, 4, BLOCK, COLS), BF16),
             pltpu.VMEM((2, 2, 2, BLOCK, QUARTER), BF16),
             pltpu.VMEM((2, 2, 2, BLOCK, COLS), BF16),
-            dma((3, 2, 8)),
-            dma((3, 2, 8)),
+            dma((4, 2, 8)),
+            dma((4, 2, 8)),
             dma((2, 2, 8)),
             dma((2, 2, 8)),
             dma((3, 4)),
             dma((3, 4)),
-            dma((15,)),
-            dma((15,)),
-            dma((9,)),
+            dma((16,)),
+            dma((16,)),
+            dma((10,)),
         ],
         compiler_params=pltpu.CompilerParams(
             collective_id=0, has_side_effects=True, vmem_limit_bytes=64 * 1024 * 1024
@@ -600,14 +668,16 @@
 
 
 def finish_kernel(
-    plan_ref, info_ref, xg_ref, fin_ref, fout_ref, rout_ref, ug_ref, dg_ref, next_ref, grad_ref, up_ref, down_ref, sem
+    plan_ref, info_ref, xg_ref, fin_ref, fout_ref, rout_ref, ug_ref, dg_ref, next_ref, grad_ref, up_ref, down_ref, up_held, down_held, sem
 ):
-    copies = [
-        pltpu.make_async_copy(ug_ref, up_ref, sem.at[0]),
-        pltpu.make_async_copy(dg_ref, down_ref, sem.at[1]),
-    ]
-    for copy in copies:
-        copy.start()
+    loads, stores = [], []
+    for n in range(4):
+        for k, (src, held, dst) in enumerate(((ug_ref, up_held, up_ref), (dg_ref, down_held, down_ref))):
+            part = pl.ds(n * (src.shape[0] // 4), src.shape[0] // 4)
+            loads.append(pltpu.make_async_copy(src.at[part], held.at[part], sem.at[0, k, n]))
+            stores.append(pltpu.make_async_copy(held.at[part], dst.at[part], sem.at[1, k, n]))
+    for load in loads:
+        load.start()
     expert = lax.axis_index("section").astype(F32)
     order, active, _ = route(plan_ref, 4, expert)
     lead = (((0,), (0,)), ((), ()))
@@ -615,6 +685,7 @@
     mine = jnp.where((order == place) & (active > 0.0), 1.0, 0.0).astype(BF16)
     theirs = jnp.where(info_ref[0:1, :] == place, 1.0, 0.0).astype(BF16)
     weight = column(info_ref[1:2, :])
+    moves = iter(zip(loads, stores))
     for half in (0, 1):
         for c in range(0, HALF, TILE):
             here, there = pl.ds(c, TILE), pl.ds(half * HALF + c, TILE)
@@ -622,8 +693,11 @@
             next_ref[:, there] = (fin_ref[:, there].astype(F32) + weight * spread).astype(BF16)
             spread = lax.dot_general(mine, rout_ref[half, :, here], lead, preferred_element_type=F32)
             grad_ref[:, there] = (xg_ref[:, there].astype(F32) + spread).astype(BF16)
-    for copy in copies:
-        copy.wait()
+            load, store = next(moves)
+            load.wait()
+            store.start()
+    for store in stores:
+        store.wait()
 
 
 def finish(plan, info, xg, fin, fout, rout, up_grad, down_grad):
@@ -634,7 +708,11 @@
         out_shape=[jax.ShapeDtypeStruct(a.shape, BF16) for a in (fin, xg, up_grad, down_grad)],
         in_specs=[vmem] * 6 + [hbm] * 2,
         out_specs=[vmem] * 2 + [hbm] * 2,
-        scratch_shapes=[pltpu.SemaphoreType.DMA((2,))],
+        scratch_shapes=[
+            pltpu.VMEM(up_grad.shape, BF16),
+            pltpu.VMEM(down_grad.shape, BF16),
+            pltpu.SemaphoreType.DMA((2, 2, 4)),
+        ],
         compiler_params=pltpu.CompilerParams(vmem_limit_bytes=64 * 1024 * 1024),
         cost_estimate=pl.CostEstimate(
             flops=150_000_000, bytes_accessed=20_000_000, transcendentals=0

time: 477 us -> 287 us (0.60)
  Pallas kernels: 472 us -> 284 us
    pallas_call x1, Pallas kernels: 196 us -> 9.38 us  [finish(): pl.pallas_call(finish_kernel, out_shape=[jax.ShapeDtypeStruct(a.shape, BF...]
where the time goes in v3:
time: 287 us
  Pallas kernels  284 us (99%)
    pallas_call x1, Pallas kernels, relay(): pl.pallas_call(kernel, out_shape=shapes, in_specs=[pl.BlockSpec(memory_sp...  274 us
    pallas_call x1, Pallas kernels, finish(): pl.pallas_call(finish_kernel, out_shape=[jax.ShapeDtypeStruct(a.shape, BF...  9.38 us

profile of v3, /device:TPU:1, one launch (start us, length us, event | category | flops | bytes accessed | tf_op | source)
XLA Modules:
  0.0 286.6 jit_solution(7526734679918624807)
XLA Ops:
  0.6 0.7 convert_bitcast_fusion
  1.3 1.3 pad_maximum_fusion.plan_ref
  2.6 274.4 %relay.1 = (bf16[128,6144]{1,0:T(8,128)(2,1)}, bf16[2,48,3072]{2,1,0:T(8,128)(2,1)}, bf16[2,48,3072]{2,1,0:T(8,128)(2,1)}, bf16[6144,256]{1,0:T(8,128)(2,1)}, bf...) custom-call(f32[8,128]{1,0:T(8,128)} %pad_maximum_fusion.plan_ref, bf16[128,6144]{1,0:T(8,128)(2,1)} %bitcast.31, ...), custom_call_target="tpu_custom_call" | custom-call | flops 28000000000 | bytes 40000000 | tf_op jit(solution)/shard_map/relay/pallas_call | solution.py:621
  277.1 9.4 %finish.1 = (bf16[128,6144]{1,0:T(8,128)(2,1)}, bf16[128,6144]{1,0:T(8,128)(2,1)}, bf16[6144,256]{1,0:T(8,128)(2,1)}, bf16[256,6144]{1,0:T(8,128)(2,1)}) custom-call(f32[8,128]{1,0:T(8,128)} %pad_maximum_fusion.plan_ref, f32[8,128]{1,0:T(8,128)} %get-tuple-element.14.info_ref, bf16[128,6144]{1,0:T(8,128)(2,1)} %bitcast.24, ...), custom_call_target="tpu_custom_call" | custom-call | flops 150000000 | bytes 20000000 | tf_op jit(solution)/shard_map/finish/pallas_call | solution.py:706

commit v4 on v3

--- a/solution.py
+++ b/solution.py
@@ -27,9 +27,9 @@
 B, G, F, X = 0, 1, 2, 3
 
 
-def route(plan_ref, base, expert):
-    hit = [plan_ref[pl.ds(base + k, 1), :] == expert for k in (0, 1)]
-    share = [plan_ref[pl.ds(base + 2 + k, 1), :] for k in (0, 1)]
+def route(ids_ref, shares_ref, expert):
+    hit = [ids_ref[pl.ds(k, 1), :] == expert for k in (0, 1)]
+    share = [shares_ref[pl.ds(k, 1), :] for k in (0, 1)]
     active = jnp.where(hit[0] | hit[1], 1.0, 0.0)
     weight = jnp.where(hit[0], share[0], 0.0) + jnp.where(hit[1], share[1], 0.0)
     earlier = lax.broadcasted_iota(jnp.int32, (TOKENS, TOKENS), 0)
@@ -41,7 +41,10 @@
 
 
 def kernel(
-    plan_ref,
+    ids_f_ref,
+    shares_f_ref,
+    ids_b_ref,
+    shares_b_ref,
     xb_ref,
     xg_ref,
     xf_ref,
@@ -156,9 +159,8 @@
         place = lax.broadcasted_iota(jnp.int32, (count, TOKENS), 0).astype(F32)
         return jnp.where((order + offset == place) & (active > 0.0), 1.0, 0.0)
 
-    expert = sec.astype(F32)
-    order_b, active_b, weight_b = route(plan_ref, 4, expert)
-    order_f, active_f, weight_f = route(plan_ref, 0, expert)
+    order_b, active_b, weight_b = route(ids_b_ref, shares_b_ref, sec)
+    order_f, active_f, weight_f = route(ids_f_ref, shares_f_ref, sec)
     shift = (CAP * zh).astype(F32)
     line = lax.broadcasted_iota(jnp.int32, (8, TOKENS), 0)
     slots_f = jnp.where(active_f > 0.0, order_f, -1.0)
@@ -539,9 +541,6 @@
     gather5(B)
     partial_up(B)
     gather4(G)
-    gather1(X)
-    gather2(X)
-    gather3(X)
     activate_fwd()
     gathered_out(F)
     wd_in.wait_recv()
@@ -552,8 +551,9 @@
     partial_back(G)
     scatter2(F)
     activate_back()
-    gather4(X)
+    gather1(X)
     down_grad()
+    gather2(X)
     kept = pl.ds(pl.multiple_of(zh * HALF, HALF), KEPT)
     dg_out = zsend(dgs.at[1, :, pl.ds(0, KEPT)], dg_ref.at[:, kept], 5)
     dg_own = keep(dgs.at[0], dg_ref.at[:, mine], 6)
@@ -563,16 +563,14 @@
     told = zsend(info, info_ref, 3, (after, me))
     back_grad()
     rows_out(G, G, wu, last)
+    gather3(X)
     scatter1(G)
     up_grad()
     ug_out = zsend(ugs.at[1], ug_ref.at[mine], 6)
     ug_own = keep(ugs.at[0], ug_ref.at[mine], 7)
-    gather5(X)
-    down_grad_extra()
-    far = pl.ds(pl.multiple_of((1 - zh) * HALF + KEPT, EXTRA), EXTRA)
-    dg_far = keep(dgs.at[1, :, pl.ds(KEPT, EXTRA)], dg_ref.at[:, far], 9)
     scatter4(F)
     scatter2(G)
+    gather4(X)
     token[B].wait_send()
     token[G].wait_send()
     token[F].wait_send()
@@ -581,6 +579,10 @@
     near_out = zsend(local.at[2], fout_ref.at[zh], 8, (after, me))
     far_out = zsend(remote.at[0], fout_ref.at[zh], 9, (after, mate))
     scatter3(G)
+    gather5(X)
+    down_grad_extra()
+    far = pl.ds(pl.multiple_of((1 - zh) * HALF + KEPT, EXTRA), EXTRA)
+    dg_far = keep(dgs.at[1, :, pl.ds(KEPT, EXTRA)], dg_ref.at[:, far], 9)
     scatter4(G)
     scatter5(G, local.at[0], local.at[1])
     row_own = keep(local.at[0], rout_ref.at[zh], 8)
@@ -607,7 +609,7 @@
     lax.fori_loop(4, 12, done, 0)
 
 
-def relay(plan, xb, xg, xf, upper, lower):
+def relay(plans, xb, xg, xf, upper, lower):
     hbm = pl.BlockSpec(memory_space=pl.ANY)
     shapes = [
         jax.ShapeDtypeStruct(xf.shape, BF16),
@@ -621,7 +623,7 @@
     return pl.pallas_call(
         kernel,
         out_shape=shapes,
-        in_specs=[pl.BlockSpec(memory_space=pltpu.VMEM)] + [hbm] * 5,
+        in_specs=[pl.BlockSpec(memory_space=pltpu.VMEM)] * 4 + [hbm] * 5,
         out_specs=[hbm] * 6,
         scratch_shapes=[
             pltpu.VMEM((8, TOKENS), F32),
@@ -658,7 +660,7 @@
             flops=28_000_000_000, bytes_accessed=40_000_000, transcendentals=2_000_000
         ),
         name="relay",
-    )(plan, xb, xg, xf, upper, lower)
+    )(*plans, xb, xg, xf, upper, lower)
 
 
 def column(line):
@@ -668,18 +670,59 @@
 
 
 def finish_kernel(
-    plan_ref, info_ref, xg_ref, fin_ref, fout_ref, rout_ref, ug_ref, dg_ref, next_ref, grad_ref, up_ref, down_ref, up_held, down_held, sem
+    ids_ref,
+    shares_ref,
+    info_ref,
+    xg_ref,
+    fin_ref,
+    fout_ref,
+    rout_ref,
+    ug_ref,
+    dg_ref,
+    next_ref,
+    grad_ref,
+    up_ref,
+    down_ref,
+    xg,
+    fin,
+    fout,
+    rout,
+    up_held,
+    down_held,
+    row_sem,
+    sem,
 ):
+    halves = [pl.ds(half * HALF, HALF) for half in (0, 1)]
+
+    def copy(src, dst, index, half):
+        return pltpu.make_async_copy(src, dst, row_sem.at[index, half])
+
+    row_loads = [
+        [
+            copy(fout_ref.at[half], fout.at[half], 0, half),
+            copy(rout_ref.at[half], rout.at[half], 1, half),
+            copy(fin_ref.at[:, halves[half]], fin.at[:, halves[half]], 2, half),
+            copy(xg_ref.at[:, halves[half]], xg.at[:, halves[half]], 3, half),
+        ]
+        for half in (0, 1)
+    ]
+    row_stores = [
+        [
+            copy(fin.at[:, halves[half]], next_ref.at[:, halves[half]], 4, half),
+            copy(xg.at[:, halves[half]], grad_ref.at[:, halves[half]], 5, half),
+        ]
+        for half in (0, 1)
+    ]
     loads, stores = [], []
     for n in range(4):
         for k, (src, held, dst) in enumerate(((ug_ref, up_held, up_ref), (dg_ref, down_held, down_ref))):
             part = pl.ds(n * (src.shape[0] // 4), src.shape[0] // 4)
             loads.append(pltpu.make_async_copy(src.at[part], held.at[part], sem.at[0, k, n]))
             stores.append(pltpu.make_async_copy(held.at[part], dst.at[part], sem.at[1, k, n]))
-    for load in loads:
+    for load in row_loads[0] + loads[:4] + row_loads[1] + loads[4:]:
         load.start()
-    expert = lax.axis_index("section").astype(F32)
-    order, active, _ = route(plan_ref, 4, expert)
+    expert = lax.axis_index("section")
+    order, active, _ = route(ids_ref, shares_ref, expert)
     lead = (((0,), (0,)), ((), ()))
     place = lax.broadcasted_iota(jnp.int32, (SLOTS, TOKENS), 0).astype(F32)
     mine = jnp.where((order == place) & (active > 0.0), 1.0, 0.0).astype(BF16)
@@ -687,38 +730,40 @@
     weight = column(info_ref[1:2, :])
     moves = iter(zip(loads, stores))
     for half in (0, 1):
+        for load in row_loads[half]:
+            load.wait()
         for c in range(0, HALF, TILE):
             here, there = pl.ds(c, TILE), pl.ds(half * HALF + c, TILE)
-            spread = lax.dot_general(theirs, fout_ref[half, :, here], lead, preferred_element_type=F32)
-            next_ref[:, there] = (fin_ref[:, there].astype(F32) + weight * spread).astype(BF16)
-            spread = lax.dot_general(mine, rout_ref[half, :, here], lead, preferred_element_type=F32)
-            grad_ref[:, there] = (xg_ref[:, there].astype(F32) + spread).astype(BF16)
+            spread = lax.dot_general(theirs, fout[half, :, here], lead, preferred_element_type=F32)
+            fin[:, there] = (fin[:, there].astype(F32) + weight * spread).astype(BF16)
+            spread = lax.dot_general(mine, rout[half, :, here], lead, preferred_element_type=F32)
+            xg[:, there] = (xg[:, there].astype(F32) + spread).astype(BF16)
             load, store = next(moves)
             load.wait()
             store.start()
-    for store in stores:
+        for store in row_stores[half]:
+            store.start()
+    for store in stores + row_stores[0] + row_stores[1]:
         store.wait()
 
 
 def finish(plan, info, xg, fin, fout, rout, up_grad, down_grad):
     hbm = pl.BlockSpec(memory_space=pl.ANY)
     vmem = pl.BlockSpec(memory_space=pltpu.VMEM)
+    held = (xg, fin, fout, rout, up_grad, down_grad)
     return pl.pallas_call(
         finish_kernel,
         out_shape=[jax.ShapeDtypeStruct(a.shape, BF16) for a in (fin, xg, up_grad, down_grad)],
-        in_specs=[vmem] * 6 + [hbm] * 2,
-        out_specs=[vmem] * 2 + [hbm] * 2,
-        scratch_shapes=[
-            pltpu.VMEM(up_grad.shape, BF16),
-            pltpu.VMEM(down_grad.shape, BF16),
-            pltpu.SemaphoreType.DMA((2, 2, 4)),
-        ],
+        in_specs=[vmem] * 3 + [hbm] * 6,
+        out_specs=[hbm] * 4,
+        scratch_shapes=[pltpu.VMEM(a.shape, BF16) for a in held]
+        + [pltpu.SemaphoreType.DMA((6, 2)), pltpu.SemaphoreType.DMA((2, 2, 4))],
         compiler_params=pltpu.CompilerParams(vmem_limit_bytes=64 * 1024 * 1024),
         cost_estimate=pl.CostEstimate(
             flops=150_000_000, bytes_accessed=20_000_000, transcendentals=0
         ),
         name="finish",
-    )(plan, info, xg, fin, fout, rout, up_grad, down_grad)
+    )(*plan, info, xg, fin, fout, rout, up_grad, down_grad)
 
 
 def body(
@@ -732,12 +777,11 @@
     up_weight,
     down_weight,
 ):
-    lines = [fwd_routes[0].T, fwd_weights[0].T, bwd_routes[0].T, bwd_weights[0].T]
-    plan = jnp.concatenate([line.astype(F32) for line in lines], axis=0)
+    plans = [fwd_routes[0].T, fwd_weights[0].T, bwd_routes[0].T, bwd_weights[0].T]
     fin, fout, rout, up_grad, down_grad, info = relay(
-        plan, bwd_input[0], out_grad[0], fwd_input[0], up_weight[0], down_weight[0]
+        plans, bwd_input[0], out_grad[0], fwd_input[0], up_weight[0], down_weight[0]
     )
-    outs = finish(plan, info, out_grad[0], fin, fout, rout, up_grad, down_grad)
+    outs = finish(plans[2:], info, out_grad[0], fin, fout, rout, up_grad, down_grad)
     return tuple(out[None] for out in outs)
 
 

time: 287 us -> 274 us (0.955)
  Pallas kernels: 284 us -> 271 us
    pallas_call x1, Pallas kernels: 274 us -> 263 us  [relay(): pl.pallas_call(kernel, out_shape=shapes, in_specs=[pl.BlockSpec(memory_sp...]
where the time goes in v4:
time: 274 us; the launch traced here: 272 us
  Pallas kernels  271 us (99%)
    pallas_call x1, Pallas kernels, relay(): pl.pallas_call(kernel, out_shape=shapes, in_specs=[pl.BlockSpec(memory_sp...  263 us
    pallas_call x1, Pallas kernels, finish(): pl.pallas_call(finish_kernel, out_shape=[jax.ShapeDtypeStruct(a.shape, BF...  7.96 us

profile of v4, /device:TPU:1, one launch (start us, length us, event | category | flops | bytes accessed | tf_op | source)
XLA Modules:
  0.0 271.8 jit_solution(15421974556880604793)
XLA Ops:
  0.6 263.0 %relay.1 = (bf16[128,6144]{1,0:T(8,128)(2,1)}, bf16[2,48,3072]{2,1,0:T(8,128)(2,1)}, bf16[2,48,3072]{2,1,0:T(8,128)(2,1)}, bf16[6144,256]{1,0:T(8,128)(2,1)}, bf...) custom-call(s32[2,128]{1,0:T(2,128)} %bitcast.35, f32[2,128]{1,0:T(2,128)} %bitcast.36, s32[2,128]{1,0:T(2,128)} %bitcast.23, ...), custom_call_target="tpu_custom_call" | custom-call | flops 28000000000 | bytes 40000000 | tf_op jit(solution)/shard_map/relay/pallas_call | solution.py:623
  263.7 8.0 %finish.1 = (bf16[128,6144]{1,0:T(8,128)(2,1)}, bf16[128,6144]{1,0:T(8,128)(2,1)}, bf16[6144,256]{1,0:T(8,128)(2,1)}, bf16[256,6144]{1,0:T(8,128)(2,1)}) custom-call(s32[2,128]{1,0:T(2,128)} %bitcast.24, f32[2,128]{1,0:T(2,128)} %bitcast.26, f32[8,128]{1,0:T(8,128)} %get-tuple-element.14.info_ref, bf16[128,6144]{1,0:T(8,128)(2,1)} %bitcast.22, ...), custom_call_target="tpu_custom_call" | custom-call | flops 150000000 | bytes 20000000 | tf_op jit(solution)/shard_map/finish/pallas_call | solution.py:754

commit v5 on v4

--- a/solution.py
+++ b/solution.py
@@ -21,6 +21,7 @@
 COLS = HALF // 2
 QUARTER = COLS // 2
 TILE = 768
+WIDE = 512
 
 EXTRA = 1536
 KEPT = HALF - EXTRA
@@ -59,6 +60,7 @@
     info,
     rows,
     extra,
+    both,
     sent,
     got,
     wu,
@@ -68,7 +70,6 @@
     part,
     peer,
     dgs,
-    ugs,
     r1,
     r2,
     r3,
@@ -175,50 +176,68 @@
 
     place_mine, place_other = place(zh), place(1 - zh)
 
+    wide_slot = lax.broadcasted_iota(jnp.int32, (BLOCK, BLOCK), 1)
+    wide_row = lax.broadcasted_iota(jnp.int32, (BLOCK, BLOCK), 0)
+
+    def place_both(s, which):
+        start = CAP if s == G else 0
+        hit = (wide_row + start == wide_slot + CAP * which) & (wide_slot >= start)
+        return jnp.where(hit & (wide_slot < start + CAP), 1.0, 0.0).astype(BF16)
+
     def pack(s, where, order, active, weight):
         for copy in fetched[s]:
             copy.wait()
-        small = selector(order, active, SLOTS, 0.0)
-        wide = selector(order, active, BLOCK, shift)
-        small_w = jnp.sum(small * weight, axis=1, keepdims=True)
-        wide_w = jnp.sum(wide * weight, axis=1, keepdims=True)
+
+        def rows_of(count, offset, half, start, width):
+            chosen = selector(order, active, count, offset)
+            value = jnp.dot(
+                chosen.astype(BF16), dgs[half, where, pl.ds(start, width)], preferred_element_type=F32
+            )
+            if s == G:
+                value = value * jnp.sum(chosen * weight, axis=1, keepdims=True)
+            return value
+
         for c in range(0, HALF, TILE):
             cols = pl.ds(c, TILE)
-            value = jnp.dot(small.astype(BF16), dgs[1 - zh, where, cols], preferred_element_type=F32)
-            if s == G:
-                value = value * small_w
-            local[s, :, cols] = value.astype(BF16)
-        copy = zsend(local.at[s], remote.at[s], s)
+            if s == F:
+                local[s, :, cols] = rows_of(SLOTS, 0.0, 1 - zh, c, TILE).astype(BF16)
+            elif s == B:
+                both[0, :, cols] = rows_of(BLOCK, 0.0, 1 - zh, c, TILE).astype(BF16)
+            else:
+                total = both[0, :, cols].astype(F32)
+                total += rows_of(BLOCK, float(CAP), 1 - zh, c, TILE)
+                both[0, :, cols] = total.astype(BF16)
+        if s == F:
+            token[F] = zsend(local.at[F], remote.at[F], F)
         if s == G:
-            for c in range(0, EXTRA, TILE):
-                value = jnp.dot(
-                    small.astype(BF16), dgs[zh, where, pl.ds(KEPT + c, TILE)], preferred_element_type=F32
-                )
-                sent[:, pl.ds(c, TILE)] = (value * small_w).astype(BF16)
+            token[G] = zsend(both.at[0], both.at[1], G)
+            for c in range(0, EXTRA, WIDE):
+                sent[:, pl.ds(c, WIDE)] = rows_of(SLOTS, 0.0, zh, KEPT + c, WIDE).astype(BF16)
             token[X] = zsend(sent, got, 15)
         for c in range(0, HALF, TILE):
-            cols = pl.ds(c, TILE)
-            value = jnp.dot(wide.astype(BF16), dgs[zh, where, cols], preferred_element_type=F32)
-            if s == G:
-                value = value * wide_w
-            rows[s, mx, my, :, cols] = value.astype(BF16)
-        return copy
+            rows[s, mx, my, :, pl.ds(c, TILE)] = rows_of(BLOCK, shift, zh, c, TILE).astype(BF16)
 
     def fill_extra():
         token[X].wait_recv()
-        for c in range(0, EXTRA, TILE):
-            cols = pl.ds(c, TILE)
+        for c in range(0, EXTRA, WIDE):
+            cols = pl.ds(c, WIDE)
             total = jnp.dot(place_other, got[:, cols], preferred_element_type=F32)
             total += jnp.dot(
-                place_mine, local[G, :, pl.ds(KEPT + c, TILE)], preferred_element_type=F32
+                place_both(G, zh), both[0, :, pl.ds(KEPT + c, WIDE)], preferred_element_type=F32
             )
             extra[mx, my, :, cols] = total.astype(BF16)
 
     def fill(s):
-        token[s].wait_recv()
+        if s != G:
+            token[G if s == B else F].wait_recv()
         for c in range(0, HALF, TILE):
             cols = pl.ds(c, TILE)
-            total = jnp.dot(place_other, remote[s, :, cols], preferred_element_type=F32)
+            if s == F:
+                total = jnp.dot(place_other, remote[s, :, cols], preferred_element_type=F32)
+            else:
+                total = jnp.dot(
+                    place_both(s, 1 - zh), both[1, :, cols], preferred_element_type=F32
+                )
             total += rows[s, mx, my, :, cols].astype(F32)
             rows[s, mx, my, :, cols] = total.astype(BF16)
 
@@ -309,8 +328,12 @@
     last = (((1,), (1,)), ((), ()))
     lead = (((0,), (0,)), ((), ()))
 
+    def turn(n):
+        return (mx + 2 + n) % 4
+
     def partial_up(s):
-        def step(i, carry):
+        def step(n, carry):
+            i = turn(n)
             block = rows[s, i].reshape(4 * BLOCK, HALF)
             for u in (0, 1):
                 value = jnp.dot(block, wu[u], preferred_element_type=F32)
@@ -321,7 +344,8 @@
         lax.fori_loop(0, 4, step, 0)
 
     def partial_back(s):
-        def step(i, carry):
+        def step(n, carry):
+            i = turn(n)
             block = rows[s, i].reshape(4 * BLOCK, HALF)
             for u in (0, 1):
                 value = lax.dot_general(block, wd[u], last, preferred_element_type=F32)
@@ -355,54 +379,46 @@
 
         lax.fori_loop(0, 4, step, 0)
 
-    def back_grad():
-        def step(i, carry):
-            pre_copy(G, i).wait_recv()
-            value = []
-            for u in (0, 1):
-                slope = part[B, i, :, pl.ds(u * UNITS, UNITS)].astype(F32)
-                value.append((whole(G, i, u) * slope).astype(BF16))
-            for u in (0, 1):
-                peer[G, i, :, pl.ds(u * UNITS, UNITS)] = value[u]
-            return carry
-
-        lax.fori_loop(0, 4, step, 0)
-
-    def activate_fwd():
-        def step(i, carry):
-            pre_copy(F, i).wait_recv()
-            hidden = []
-            for u in (0, 1):
-                pre = whole(F, i, u)
-                hidden.append((pre * sigmoid(pre)).astype(BF16))
-            for u in (0, 1):
-                peer[F, i, :, pl.ds(u * UNITS, UNITS)] = hidden[u]
-            return carry
-
-        lax.fori_loop(0, 4, step, 0)
+    def back_grad(i):
+        pre_copy(G, i).wait_recv()
+        value = []
+        for u in (0, 1):
+            slope = part[B, i, :, pl.ds(u * UNITS, UNITS)].astype(F32)
+            value.append((whole(G, i, u) * slope).astype(BF16))
+        for u in (0, 1):
+            peer[G, i, :, pl.ds(u * UNITS, UNITS)] = value[u]
+
+    def activate_fwd(i):
+        pre_copy(F, i).wait_recv()
+        hidden = []
+        for u in (0, 1):
+            pre = whole(F, i, u)
+            hidden.append((pre * sigmoid(pre)).astype(BF16))
+        for u in (0, 1):
+            peer[F, i, :, pl.ds(u * UNITS, UNITS)] = hidden[u]
 
     def down_grad():
         for u, width in ((1, KEPT), (0, HALF)):
             def step(c, carry):
-                cols = pl.ds(pl.multiple_of(c * TILE, TILE), TILE)
+                cols = pl.ds(pl.multiple_of(c * WIDE, WIDE), WIDE)
                 left = peer[B, :, :, pl.ds(u * UNITS, UNITS)].reshape(16 * BLOCK, UNITS)
-                right = rows[G, :, :, :, cols].reshape(16 * BLOCK, TILE)
+                right = rows[G, :, :, :, cols].reshape(16 * BLOCK, WIDE)
                 value = lax.dot_general(left, right, lead, preferred_element_type=F32)
                 dgs[u, :, cols] = value.astype(BF16)
                 return carry
 
-            lax.fori_loop(0, width // TILE, step, 0)
+            lax.fori_loop(0, width // WIDE, step, 0)
 
     def down_grad_extra():
         def step(c, carry):
-            start = pl.multiple_of(c * TILE, TILE)
+            start = pl.multiple_of(c * WIDE, WIDE)
             left = peer[B, :, :, pl.ds(0, UNITS)].reshape(16 * BLOCK, UNITS)
-            right = extra[:, :, :, pl.ds(start, TILE)].reshape(16 * BLOCK, TILE)
+            right = extra[:, :, :, pl.ds(start, WIDE)].reshape(16 * BLOCK, WIDE)
             value = lax.dot_general(left, right, lead, preferred_element_type=F32)
-            dgs[1, :, pl.ds(KEPT + start, TILE)] = value.astype(BF16)
+            dgs[1, :, pl.ds(KEPT + start, WIDE)] = value.astype(BF16)
             return carry
 
-        lax.fori_loop(0, EXTRA // TILE, step, 0)
+        lax.fori_loop(0, EXTRA // WIDE, step, 0)
 
     def up_grad():
         def step(c, carry):
@@ -411,29 +427,37 @@
             for u in (0, 1):
                 right = peer[G, :, :, pl.ds(u * UNITS, UNITS)].reshape(16 * BLOCK, UNITS)
                 value = lax.dot_general(left, right, lead, preferred_element_type=F32)
-                ugs[u, cols, :] = value.astype(BF16)
+                wu[u, cols, :] = value.astype(BF16)
             return carry
 
         lax.fori_loop(0, HALF // TILE, step, 0)
 
-    def rows_out(s, source, weights, dims):
-        def step(n, carry):
-            i = n // (HALF // TILE)
-            c = n % (HALF // TILE)
-            cols = pl.ds(pl.multiple_of(c * TILE, TILE), TILE)
-            total = None
-            for u in (0, 1):
-                left = peer[source, i, :, pl.ds(u * UNITS, UNITS)]
-                right = weights[u, cols, :] if dims == last else weights[u, :, cols]
-                if dims == last:
-                    value = lax.dot_general(left, right, last, preferred_element_type=F32)
-                else:
-                    value = jnp.dot(left, right, preferred_element_type=F32)
-                total = value if total is None else total + value
-            rows[s, i, :, :, cols] = total.astype(BF16).reshape(4, BLOCK, TILE)
+    def rows_out(s, activate, weights, dims):
+        def column(n, carry):
+            i = turn(n)
+            activate(i)
+
+            def step(c, carry):
+                cols = pl.ds(pl.multiple_of(c * TILE, TILE), TILE)
+                total = None
+                for u in (0, 1):
+                    left = peer[s, i, :, pl.ds(u * UNITS, UNITS)]
+                    right = weights[u, cols, :] if dims == last else weights[u, :, cols]
+                    if dims == last:
+                        value = lax.dot_general(left, right, last, preferred_element_type=F32)
+                    else:
+                        value = jnp.dot(left, right, preferred_element_type=F32)
+                    total = value if total is None else total + value
+                rows[s, i, :, :, cols] = total.astype(BF16).reshape(4, BLOCK, TILE)
+                return carry
+
+            lax.fori_loop(0, HALF // TILE, step, 0)
             return carry
 
-        lax.fori_loop(0, 4 * (HALF // TILE), step, 0)
+        lax.fori_loop(0, 1, column, 0)
+        scatter1(s, 1)
+        lax.fori_loop(1, 4, column, 0)
+        scatter1(s, 0)
 
     scatters = {}
 
@@ -460,14 +484,13 @@
             total += source[...].astype(F32)
         rows[s, x, y, :, pl.ds(h * COLS + start, width)] = total.astype(BF16)
 
-    def scatter1(s):
-        for h in (0, 1):
-            far = second[h] + 2
-            ssend(s, h, 0, g4(s, h, far, 0, QUARTER), r1.at[s - 1, h, 0], dev2(h, 1))
-            ssend(s, h, 1, g4(s, h, far, QUARTER, QUARTER), r1.at[s - 1, h, 1], dev2(h, -1))
+    def scatter1(s, h):
+        far = second[h] + 2
+        ssend(s, h, 0, g4(s, h, far, 0, QUARTER), r1.at[s - 1, h, 0], dev2(h, 1))
+        ssend(s, h, 1, g4(s, h, far, QUARTER, QUARTER), r1.at[s - 1, h, 1], dev2(h, -1))
 
     def scatter2(s):
-        for h in (0, 1):
+        for h in (1, 0):
             scatters[s, h, 0].wait_recv()
             add4(s, h, second[h] + 1, 0, QUARTER, [r1.at[s - 1, h, 0]])
             ssend(s, h, 2, g4(s, h, second[h] + 1, 0, COLS), r2.at[s - 1, h, 0], dev2(h, 1))
@@ -508,13 +531,13 @@
                 place_other, block, lead, preferred_element_type=F32
             ).astype(BF16)
 
-    token[F] = pack(F, upper, order_f, active_f, weight_f)
+    pack(F, upper, order_f, active_f, weight_f)
     fetched[G] = fetch(xg_ref, upper, 0)
-    token[B] = pack(B, lower, order_b, active_b, weight_b)
+    pack(B, lower, order_b, active_b, weight_b)
     wu_in.append(up_part(1))
     wu_own = keep(up_ref.at[mine], wu.at[0], 4)
     wd_own = keep(down_ref.at[:, mine], wd.at[0], 5)
-    token[G] = pack(G, upper, order_b, active_b, weight_b)
+    pack(G, upper, order_b, active_b, weight_b)
     wu_in.append(up_part(2))
     wu_in.append(up_part(3))
     fill(F)
@@ -541,15 +564,14 @@
     gather5(B)
     partial_up(B)
     gather4(G)
-    activate_fwd()
     gathered_out(F)
     wd_in.wait_recv()
     wd_own.wait()
-    rows_out(F, F, wd, None)
-    scatter1(F)
+    rows_out(F, activate_fwd, wd, None)
     gather5(G)
     partial_back(G)
     scatter2(F)
+    fin = zsend(xf_ref, fin_ref, 10, (after, me))
     activate_back()
     gather1(X)
     down_grad()
@@ -559,19 +581,15 @@
     dg_own = keep(dgs.at[0], dg_ref.at[:, mine], 6)
     gathered_out(G)
     scatter3(F)
-    fin = zsend(xf_ref, fin_ref, 10, (after, me))
     told = zsend(info, info_ref, 3, (after, me))
-    back_grad()
-    rows_out(G, G, wu, last)
+    rows_out(G, back_grad, wu, last)
     gather3(X)
-    scatter1(G)
     up_grad()
-    ug_out = zsend(ugs.at[1], ug_ref.at[mine], 6)
-    ug_own = keep(ugs.at[0], ug_ref.at[mine], 7)
+    ug_out = zsend(wu.at[1], ug_ref.at[mine], 6)
+    ug_own = keep(wu.at[0], ug_ref.at[mine], 7)
+    scatter2(G)
     scatter4(F)
-    scatter2(G)
     gather4(X)
-    token[B].wait_send()
     token[G].wait_send()
     token[F].wait_send()
     token[X].wait_send()
@@ -579,14 +597,14 @@
     near_out = zsend(local.at[2], fout_ref.at[zh], 8, (after, me))
     far_out = zsend(remote.at[0], fout_ref.at[zh], 9, (after, mate))
     scatter3(G)
-    gather5(X)
-    down_grad_extra()
-    far = pl.ds(pl.multiple_of((1 - zh) * HALF + KEPT, EXTRA), EXTRA)
-    dg_far = keep(dgs.at[1, :, pl.ds(KEPT, EXTRA)], dg_ref.at[:, far], 9)
     scatter4(G)
     scatter5(G, local.at[0], local.at[1])
     row_own = keep(local.at[0], rout_ref.at[zh], 8)
     row_out = zsend(local.at[1], rout_ref.at[zh], 7)
+    gather5(X)
+    down_grad_extra()
+    far = pl.ds(pl.multiple_of((1 - zh) * HALF + KEPT, WIDE), EXTRA)
+    dg_far = keep(dgs.at[1, :, pl.ds(KEPT, EXTRA)], dg_ref.at[:, far], 9)
 
     for copy in (dg_own, dg_far, ug_own, row_own):
         copy.wait()
@@ -629,6 +647,7 @@
             pltpu.VMEM((8, TOKENS), F32),
             pltpu.VMEM((3, 4, 4, BLOCK, HALF), BF16),
             pltpu.VMEM((4, 4, BLOCK, EXTRA), BF16),
+            pltpu.VMEM((2, BLOCK, HALF), BF16),
             pltpu.VMEM((SLOTS, EXTRA), BF16),
             pltpu.VMEM((SLOTS, EXTRA), BF16),
             pltpu.VMEM((2, HALF, UNITS), BF16),
@@ -638,7 +657,6 @@
             pltpu.VMEM((3, 4, 4 * BLOCK, 2 * UNITS), BF16),
             pltpu.VMEM((3, 4, 4 * BLOCK, 2 * UNITS), BF16),
             pltpu.VMEM((2, UNITS, HALF), BF16),
-            pltpu.VMEM((2, HALF, UNITS), BF16),
             pltpu.VMEM((2, 2, 2, 4, BLOCK, QUARTER), BF16),
             pltpu.VMEM((2, 2, 2, 4, BLOCK, COLS), BF16),
             pltpu.VMEM((2, 2, 2, BLOCK, QUARTER), BF16),

time: 274 us -> 273 us (level)
  Pallas kernels: 271 us -> 268 us
where the time goes in v5:
time: 273 us; the launch traced here: 269 us
  Pallas kernels  268 us (98%)
    pallas_call x1, Pallas kernels, relay(): pl.pallas_call(kernel, out_shape=shapes, in_specs=[pl.BlockSpec(memory_sp...  260 us
    pallas_call x1, Pallas kernels, finish(): pl.pallas_call(finish_kernel, out_shape=[jax.ShapeDtypeStruct(a.shape, BF...  7.96 us

profile of v5, /device:TPU:1, one launch (start us, length us, event | category | flops | bytes accessed | tf_op | source)
XLA Modules:
  0.0 269.2 jit_solution(529756884278997021)
XLA Ops:
  0.6 260.4 %relay.1 = (bf16[128,6144]{1,0:T(8,128)(2,1)}, bf16[2,48,3072]{2,1,0:T(8,128)(2,1)}, bf16[2,48,3072]{2,1,0:T(8,128)(2,1)}, bf16[6144,256]{1,0:T(8,128)(2,1)}, bf...) custom-call(s32[2,128]{1,0:T(2,128)} %bitcast.35, f32[2,128]{1,0:T(2,128)} %bitcast.36, s32[2,128]{1,0:T(2,128)} %bitcast.23, ...), custom_call_target="tpu_custom_call" | custom-call | flops 28000000000 | bytes 40000000 | tf_op jit(solution)/shard_map/relay/pallas_call | solution.py:641
  261.1 8.0 %finish.1 = (bf16[128,6144]{1,0:T(8,128)(2,1)}, bf16[128,6144]{1,0:T(8,128)(2,1)}, bf16[6144,256]{1,0:T(8,128)(2,1)}, bf16[256,6144]{1,0:T(8,128)(2,1)}) custom-call(s32[2,128]{1,0:T(2,128)} %bitcast.24, f32[2,128]{1,0:T(2,128)} %bitcast.26, f32[8,128]{1,0:T(8,128)} %get-tuple-element.14.info_ref, bf16[128,6144]{1,0:T(8,128)(2,1)} %bitcast.22, ...), custom_call_target="tpu_custom_call" | custom-call | flops 150000000 | bytes 20000000 | tf_op jit(solution)/shard_map/finish/pallas_call | solution.py:772

commit v6 on v5

--- a/solution.py
+++ b/solution.py
@@ -737,7 +737,7 @@
             part = pl.ds(n * (src.shape[0] // 4), src.shape[0] // 4)
             loads.append(pltpu.make_async_copy(src.at[part], held.at[part], sem.at[0, k, n]))
             stores.append(pltpu.make_async_copy(held.at[part], dst.at[part], sem.at[1, k, n]))
-    for load in row_loads[0] + loads[:4] + row_loads[1] + loads[4:]:
+    for load in row_loads[0] + row_loads[1] + loads:
         load.start()
     expert = lax.axis_index("section")
     order, active, _ = route(ids_ref, shares_ref, expert)

time: 273 us -> 273 us (level)
  no operation moved by 1% of the time
where the time goes in v6:
time: 273 us; the launch traced here: 269 us
  Pallas kernels  268 us (98%)
    pallas_call x1, Pallas kernels, relay(): pl.pallas_call(kernel, out_shape=shapes, in_specs=[pl.BlockSpec(memory_sp...  260 us
    pallas_call x1, Pallas kernels, finish(): pl.pallas_call(finish_kernel, out_shape=[jax.ShapeDtypeStruct(a.shape, BF...  7.96 us

profile of v6, /device:TPU:1, one launch (start us, length us, event | category | flops | bytes accessed | tf_op | source)
XLA Modules:
  0.0 269.2 jit_solution(529756884278997021)
XLA Ops:
  0.6 260.4 %relay.1 = (bf16[128,6144]{1,0:T(8,128)(2,1)}, bf16[2,48,3072]{2,1,0:T(8,128)(2,1)}, bf16[2,48,3072]{2,1,0:T(8,128)(2,1)}, bf16[6144,256]{1,0:T(8,128)(2,1)}, bf...) custom-call(s32[2,128]{1,0:T(2,128)} %bitcast.35, f32[2,128]{1,0:T(2,128)} %bitcast.36, s32[2,128]{1,0:T(2,128)} %bitcast.23, ...), custom_call_target="tpu_custom_call" | custom-call | flops 28000000000 | bytes 40000000 | tf_op jit(solution)/shard_map/relay/pallas_call | solution.py:641
  261.1 8.0 %finish.1 = (bf16[128,6144]{1,0:T(8,128)(2,1)}, bf16[128,6144]{1,0:T(8,128)(2,1)}, bf16[6144,256]{1,0:T(8,128)(2,1)}, bf16[256,6144]{1,0:T(8,128)(2,1)}) custom-call(s32[2,128]{1,0:T(2,128)} %bitcast.24, f32[2,128]{1,0:T(2,128)} %bitcast.26, f32[8,128]{1,0:T(8,128)} %get-tuple-element.14.info_ref, bf16[128,6144]{1,0:T(8,128)(2,1)} %bitcast.22, ...), custom_call_target="tpu_custom_call" | custom-call | flops 150000000 | bytes 20000000 | tf_op jit(solution)/shard_map/finish/pallas_call | solution.py:772
